TPU v7x, 32 devices: a whole 2x2x4 slice. The times are simulated.
32 devices in a mesh: gx: 8 (over z, y), gy: 4 (over x, core).
Axes of the slice: x: 2, y: 2, z: 4, core: 2. Of those that a mesh axis runs over, the one named last changes fastest.
Arguments:
- position: float32 [3, 524288], P(None, ('gx', 'gy')), may hold values from -3 to 295.6
- velocity: float32 [3, 524288], P(None, ('gx', 'gy')), may hold values from -0.6 to 0.6
- mass: float32 [524288], P(('gx', 'gy')), may hold values from 0.01 to 0.04
- smoothing: float32 [524288], P(('gx', 'gy')), may hold values from 0.8 to 1.25
- energy: float32 [524288], P(('gx', 'gy')), may hold values from 0.35 to 5.6
- live_blocks: int32 [32], P(('gx', 'gy')), may hold values from 64 to 128, as said below
- send_list: int32 [32, 6, 12], P(('gx', 'gy')), may hold values from 0 to 23, as said below
- nbr_list: int32 [4096, 8], P(('gx', 'gy')), may hold values from 0 to 199, as said below
- nbr_count: int32 [4096], P(('gx', 'gy')), may hold values from 4 to 8
Outputs:
- density: float32 [524288], P(('gx', 'gy'))
- kick: float32 [3, 524288], P(None, ('gx', 'gy'))
- heating: float32 [524288], P(('gx', 'gy'))
Inputs may be any that keep to these rules, and one draw needn't show every extreme that they name: `live_blocks`: the live blocks of a domain are its first ones; some domain has all 128 live and some exactly 64. `send_list`: entries are block indices within the sending domain, all among its first 24 blocks and distinct within one peer list; entry 0 of every list p below 4 is block 0. List p below 4 goes to the domain of fine index p in the same segment, list 4 to the previous segment's domain of the same fine index, list 4 + 1 to the next one's. `nbr_list`: entry 0 of a block's list is the block itself; the others are distinct slots: a live block of the own domain, or a slot 128 + p * 12 + s received from another domain, where p is not the domain's own fine index, p = 4 only if a previous segment exists and p = 5 only if a next one exists.
All inputs are finite; a program needn't handle non-finite values.
Results may differ from a plain program's by a relative error of at most 0.0003.
Values sent between devices are 32-bit elements; how exact they have to be, the bound alone decides.
A program may use at most 64 MiB of HBM per device.

v0:
```python
import math

import jax
import jax.numpy as jnp
from jax import lax
from jax.sharding import PartitionSpec as P

GAMMA = 5.0 / 3.0
VISC_ALPHA = 1.0
VISC_BETA = 2.0
ETA_SQUARED = 0.01
COURANT = 0.3
KERNEL_NORM = 21.0 / (16.0 * math.pi)
FAR_STEP = 1e30


def padded(array, sides, width):
    for axis, dim in sides:
        size, length = (lax.axis_size(axis), array.shape[dim])
        up = [(i, (i + 1) % size) for i in range(size - 1)]
        down = [(j, i) for i, j in up]
        last = lax.slice_in_dim(array, length - width, length, axis=dim)
        first = lax.slice_in_dim(array, 0, width, axis=dim)
        before = lax.ppermute(last, axis, up)
        after = lax.ppermute(first, axis, down)
        array = jnp.concatenate([before, array, after], axis=dim)
    return array


def kernel_sum(target_pos, target_smooth, source_pos, source_weight):
    squares = sum(
        (
            (target_pos[component][:, None, :] - source_pos[component][:, :, None]) ** 2
            for component in range(3)
        )
    )
    ratio = jnp.sqrt(squares) / target_smooth[:, None, :]
    taper = jnp.maximum(1.0 - 0.5 * ratio, 0.0)
    profile = taper**4 * (1.0 + 2.0 * ratio)
    total = jnp.sum(source_weight[:, :, None] * profile, axis=1)
    return KERNEL_NORM / target_smooth**3 * total


def pressure_terms(dens, thermal):
    return ((GAMMA - 1.0) * thermal / dens, jnp.sqrt(GAMMA * (GAMMA - 1.0) * thermal))


def force_sum(target, source, source_weight, source_valid):
    target_pos, target_vel, target_smooth, target_dens, target_press, target_sound = target
    source_pos, source_vel, source_smooth, source_dens, source_press, source_sound = source
    offsets = [
        target_pos[component][:, None, :] - source_pos[component][:, :, None]
        for component in range(3)
    ]
    moving = [
        target_vel[component][:, None, :] - source_vel[component][:, :, None]
        for component in range(3)
    ]
    squares = offsets[0] * offsets[0] + offsets[1] * offsets[1] + offsets[2] * offsets[2]
    closing = offsets[0] * moving[0] + offsets[1] * moving[1] + offsets[2] * moving[2]
    mean_smooth = 0.5 * (target_smooth[:, None, :] + source_smooth[:, :, None])
    taper = jnp.maximum(1.0 - 0.5 * jnp.sqrt(squares) / mean_smooth, 0.0)
    slope = -5.0 * KERNEL_NORM * taper**3 / mean_smooth**5
    approach = (
        mean_smooth
        * jnp.minimum(closing, 0.0)
        / (squares + ETA_SQUARED * mean_smooth * mean_smooth)
    )
    mean_sound = 0.5 * (target_sound[:, None, :] + source_sound[:, :, None])
    mean_dens = 0.5 * (target_dens[:, None, :] + source_dens[:, :, None])
    visc = (-VISC_ALPHA * mean_sound * approach + VISC_BETA * approach * approach) / mean_dens
    coef = (
        source_weight[:, :, None]
        * (target_press[:, None, :] + source_press[:, :, None] + visc)
        * slope
    )
    accel = jnp.stack([-jnp.sum(coef * offset, axis=1) for offset in offsets])
    rate = 0.5 * jnp.sum(coef * closing, axis=1)
    signal = jnp.max(jnp.where(source_valid[:, :, None], -approach, 0.0), axis=1)
    return (accel, rate, signal)


def shards(
    position, velocity, mass, smoothing, energy, live_blocks, send_list, nbr_list, nbr_count
):
    peer_count = lax.axis_size("gy")
    block_count = nbr_count.shape[0]
    block_size = mass.shape[0] // block_count
    slot_count = send_list.shape[2]
    list_width = nbr_list.shape[1]
    places = position.reshape(3, block_count, block_size)
    speeds = velocity.reshape(3, block_count, block_size)
    masses = mass.reshape(block_count, block_size)
    smooth = smoothing.reshape(block_count, block_size)
    thermal = energy.reshape(block_count, block_size)
    to_fine = send_list[0, :peer_count].reshape(-1)
    to_segment = send_list[0, peer_count:].reshape(-1)
    stack = jnp.concatenate([places, masses[None], smooth[None]], axis=0)
    height = stack.shape[0]
    outgoing = stack[:, to_fine].reshape(height, peer_count, slot_count, block_size)
    arrived = lax.all_to_all(outgoing, "gy", split_axis=1, concat_axis=1, tiled=True)
    border = padded(stack[:, to_segment], (("gx", 1),), slot_count)
    first = jnp.concatenate(
        [
            arrived.reshape(height, peer_count * slot_count, block_size),
            border[:, :slot_count],
            border[:, 3 * slot_count :],
        ],
        axis=1,
    )
    ghost_pos = first[0:3]
    ghost_mass = first[3]
    ghost_smooth = first[4]
    wide_pos = jnp.concatenate([places, ghost_pos], axis=1)
    wide_mass = jnp.concatenate([masses, ghost_mass], axis=0)
    group = min(block_count, 8)
    turns = block_count // group
    usable = jnp.arange(list_width, dtype=jnp.int32)[None, :] < nbr_count[:, None]
    usable_rows = jnp.repeat(usable, block_size, axis=1).reshape(
        turns, group, list_width * block_size
    )
    grouped_lists = nbr_list.reshape(turns, group, list_width)

    def density_group(inputs):
        chosen, allowed, target_pos, target_smooth = inputs
        source_pos = wide_pos[:, chosen].reshape(3, group, list_width * block_size)
        weight = jnp.where(allowed, wide_mass[chosen].reshape(group, list_width * block_size), 0.0)
        return kernel_sum(target_pos, target_smooth, source_pos, weight)

    grouped_pos = jnp.moveaxis(places.reshape(3, turns, group, block_size), 1, 0)
    rho = lax.map(
        density_group,
        (grouped_lists, usable_rows, grouped_pos, smooth.reshape(turns, group, block_size)),
    )
    rho = rho.reshape(block_count, block_size)
    press, sound = pressure_terms(rho, thermal)
    stack = jnp.concatenate([rho[None], speeds, thermal[None]], axis=0)
    height = stack.shape[0]
    outgoing = stack[:, to_fine].reshape(height, peer_count, slot_count, block_size)
    arrived = lax.all_to_all(outgoing, "gy", split_axis=1, concat_axis=1, tiled=True)
    border = padded(stack[:, to_segment], (("gx", 1),), slot_count)
    second = jnp.concatenate(
        [
            arrived.reshape(height, peer_count * slot_count, block_size),
            border[:, :slot_count],
            border[:, 3 * slot_count :],
        ],
        axis=1,
    )
    ghost_rho = second[0]
    ghost_vel = second[1:4]
    ghost_press, ghost_sound = pressure_terms(ghost_rho, second[4])
    own_table = jnp.concatenate(
        [places, speeds, masses[None], smooth[None], rho[None], press[None], sound[None]], axis=0
    )
    ghost_table = jnp.concatenate(
        [
            ghost_pos,
            ghost_vel,
            ghost_mass[None],
            ghost_smooth[None],
            ghost_rho[None],
            ghost_press[None],
            ghost_sound[None],
        ],
        axis=0,
    )
    wide_table = jnp.concatenate([own_table, ghost_table], axis=1)
    row_count = own_table.shape[0]

    def force_group(inputs):
        chosen, allowed, target_rows = inputs
        source_rows = wide_table[:, chosen].reshape(row_count, group, list_width * block_size)
        weight = jnp.where(allowed, source_rows[6], 0.0)
        target = (
            target_rows[0:3],
            target_rows[3:6],
            target_rows[7],
            target_rows[8],
            target_rows[9],
            target_rows[10],
        )
        source = (
            source_rows[0:3],
            source_rows[3:6],
            source_rows[7],
            source_rows[8],
            source_rows[9],
            source_rows[10],
        )
        return force_sum(target, source, weight, allowed)

    grouped_rows = jnp.moveaxis(own_table.reshape(row_count, turns, group, block_size), 1, 0)
    accel, rate, signal = lax.map(force_group, (grouped_lists, usable_rows, grouped_rows))
    accel = jnp.moveaxis(accel, 1, 0).reshape(3, block_count, block_size)
    rate = rate.reshape(block_count, block_size)
    signal = signal.reshape(block_count, block_size)
    alive = jnp.arange(block_count, dtype=jnp.int32)[:, None] < live_blocks[0]
    alive = jnp.broadcast_to(alive, (block_count, block_size))
    step = COURANT * smooth / (sound + 1.2 * (VISC_ALPHA * sound + VISC_BETA * signal))
    local_least = jnp.min(jnp.where(alive, step, FAR_STEP))
    timestep = lax.pmin(local_least, ("gx", "gy"))
    density = jnp.where(alive, rho, 0.0).reshape(-1)
    kick = jnp.where(alive[None], timestep * accel, 0.0).reshape(3, -1)
    heating = jnp.where(alive, timestep * rate, 0.0).reshape(-1)
    return (density, kick, heating)


def solution(mesh):
    return jax.shard_map(
        shards,
        mesh=mesh,
        in_specs=(
            P(None, ("gx", "gy")),
            P(None, ("gx", "gy")),
            P(("gx", "gy")),
            P(("gx", "gy")),
            P(("gx", "gy")),
            P(("gx", "gy")),
            P(("gx", "gy"), None, None),
            P(("gx", "gy"), None),
            P(("gx", "gy")),
        ),
        out_specs=(P(("gx", "gy")), P(None, ("gx", "gy")), P(("gx", "gy"))),
        check_vma=False,
    )
```

profile of v0, /device:TPU:0, one launch (start us, length us, event | category | flops | bytes accessed | tf_op | source)
XLA Modules:
  0.0 457.8 jit_solution(14153921936731087826)
XLA Ops:
  2.3 1.2 pad_maximum_fusion.1
  4.1 1.3 collective-permute-start.1
  5.4 5.5 %collective-permute-start = (f32[5,12,128]{2,0,1:T(8,128)S(1)}, f32[5,12,128]{2,0,1:T(8,128)S(1)}, u32[]{:S(2)}, u32[]{:S(2)}) collective-permute-start(f32[5,12,128]{2,0,1:T(8,128)S(1)} %get-tuple-element.279), channel_id=1, source_target_pairs={{0,4},{4,8},{8,12},{12,16},{16,20},{20,24},{24,28},{1,5},{5,9},{9,... | collective-permute-start | bytes 92168 | tf_op jit(solution)/shard_map/ppermute | solution.py:24
  12.3 3.3 all-to-all-start
  19.5 1.0 all-to-all-done
  20.9 108.2 %while.26 = (s32[]{:T(128)}, f32[16,8,128]{2,1,0:T(8,128)S(1)}, f32[16,8,128]{2,1,0:T(8,128)S(1)}, pred[16,8,1024]{2,1,0:T(8,128)(4,1)S(1)}, s32[16,8,8]{2,1,0:T...) while((s32[]{:T(128)}, f32[16,8,128]{2,1,0:T(8,128)S(1)}, ...), condition=%wide.region_2.3_spmd, body=%wide.region_0.2_spmd.sunk | while | flops 19935424 | bytes 1021817 | solution.py:131
  22.7 5.0 %multiply_reduce_fusion.4 = f32[8,128]{1,0:T(8,128)S(1)} fusion(f32[8,128]{1,0:T(8,128)S(1)} %dynamic-slice_bitcast_fusion.8, f32[8,1024]{1,0:T(8,128)S(1)} %get-tuple-element.419, f32[8,128]{1,0:T(8,128)S(1)} %get-tuple-element.420, f32[8,1024]{1,0:T(8,128)S(1)} %get-tuple-element.421, f32[8,128]{1,0:T(8,128)S(1)} %get-tuple-element.422, ...), kind=kLoop, calls=%fused_computation.7.clone.1 | loop fusion | flops 19921920 | bytes 151552 | tf_op jit(solution)/shard_map/while/body/eval_jaxpr/reduce_sum | solution.py:40
  29.4 5.0 %multiply_reduce_fusion.4 = f32[8,128]{1,0:T(8,128)S(1)} fusion(f32[8,128]{1,0:T(8,128)S(1)} %dynamic-slice_bitcast_fusion.8, f32[8,1024]{1,0:T(8,128)S(1)} %get-tuple-element.419, f32[8,128]{1,0:T(8,128)S(1)} %get-tuple-element.420, f32[8,1024]{1,0:T(8,128)S(1)} %get-tuple-element.421, f32[8,128]{1,0:T(8,128)S(1)} %get-tuple-element.422, ...), kind=kLoop, calls=%fused_computation.7.clone.1 | loop fusion | flops 19921920 | bytes 151552 | tf_op jit(solution)/shard_map/while/body/eval_jaxpr/reduce_sum | solution.py:40
  36.2 5.0 %multiply_reduce_fusion.4 = f32[8,128]{1,0:T(8,128)S(1)} fusion(f32[8,128]{1,0:T(8,128)S(1)} %dynamic-slice_bitcast_fusion.8, f32[8,1024]{1,0:T(8,128)S(1)} %get-tuple-element.419, f32[8,128]{1,0:T(8,128)S(1)} %get-tuple-element.420, f32[8,1024]{1,0:T(8,128)S(1)} %get-tuple-element.421, f32[8,128]{1,0:T(8,128)S(1)} %get-tuple-element.422, ...), kind=kLoop, calls=%fused_computation.7.clone.1 | loop fusion | flops 19921920 | bytes 151552 | tf_op jit(solution)/shard_map/while/body/eval_jaxpr/reduce_sum | solution.py:40
  43.0 5.0 %multiply_reduce_fusion.4 = f32[8,128]{1,0:T(8,128)S(1)} fusion(f32[8,128]{1,0:T(8,128)S(1)} %dynamic-slice_bitcast_fusion.8, f32[8,1024]{1,0:T(8,128)S(1)} %get-tuple-element.419, f32[8,128]{1,0:T(8,128)S(1)} %get-tuple-element.420, f32[8,1024]{1,0:T(8,128)S(1)} %get-tuple-element.421, f32[8,128]{1,0:T(8,128)S(1)} %get-tuple-element.422, ...), kind=kLoop, calls=%fused_computation.7.clone.1 | loop fusion | flops 19921920 | bytes 151552 | tf_op jit(solution)/shard_map/while/body/eval_jaxpr/reduce_sum | solution.py:40
  49.7 5.0 %multiply_reduce_fusion.4 = f32[8,128]{1,0:T(8,128)S(1)} fusion(f32[8,128]{1,0:T(8,128)S(1)} %dynamic-slice_bitcast_fusion.8, f32[8,1024]{1,0:T(8,128)S(1)} %get-tuple-element.419, f32[8,128]{1,0:T(8,128)S(1)} %get-tuple-element.420, f32[8,1024]{1,0:T(8,128)S(1)} %get-tuple-element.421, f32[8,128]{1,0:T(8,128)S(1)} %get-tuple-element.422, ...), kind=kLoop, calls=%fused_computation.7.clone.1 | loop fusion | flops 19921920 | bytes 151552 | tf_op jit(solution)/shard_map/while/body/eval_jaxpr/reduce_sum | solution.py:40
  56.5 5.0 %multiply_reduce_fusion.4 = f32[8,128]{1,0:T(8,128)S(1)} fusion(f32[8,128]{1,0:T(8,128)S(1)} %dynamic-slice_bitcast_fusion.8, f32[8,1024]{1,0:T(8,128)S(1)} %get-tuple-element.419, f32[8,128]{1,0:T(8,128)S(1)} %get-tuple-element.420, f32[8,1024]{1,0:T(8,128)S(1)} %get-tuple-element.421, f32[8,128]{1,0:T(8,128)S(1)} %get-tuple-element.422, ...), kind=kLoop, calls=%fused_computation.7.clone.1 | loop fusion | flops 19921920 | bytes 151552 | tf_op jit(solution)/shard_map/while/body/eval_jaxpr/reduce_sum | solution.py:40
  63.2 5.0 %multiply_reduce_fusion.4 = f32[8,128]{1,0:T(8,128)S(1)} fusion(f32[8,128]{1,0:T(8,128)S(1)} %dynamic-slice_bitcast_fusion.8, f32[8,1024]{1,0:T(8,128)S(1)} %get-tuple-element.419, f32[8,128]{1,0:T(8,128)S(1)} %get-tuple-element.420, f32[8,1024]{1,0:T(8,128)S(1)} %get-tuple-element.421, f32[8,128]{1,0:T(8,128)S(1)} %get-tuple-element.422, ...), kind=kLoop, calls=%fused_computation.7.clone.1 | loop fusion | flops 19921920 | bytes 151552 | tf_op jit(solution)/shard_map/while/body/eval_jaxpr/reduce_sum | solution.py:40
  70.0 5.0 %multiply_reduce_fusion.4 = f32[8,128]{1,0:T(8,128)S(1)} fusion(f32[8,128]{1,0:T(8,128)S(1)} %dynamic-slice_bitcast_fusion.8, f32[8,1024]{1,0:T(8,128)S(1)} %get-tuple-element.419, f32[8,128]{1,0:T(8,128)S(1)} %get-tuple-element.420, f32[8,1024]{1,0:T(8,128)S(1)} %get-tuple-element.421, f32[8,128]{1,0:T(8,128)S(1)} %get-tuple-element.422, ...), kind=kLoop, calls=%fused_computation.7.clone.1 | loop fusion | flops 19921920 | bytes 151552 | tf_op jit(solution)/shard_map/while/body/eval_jaxpr/reduce_sum | solution.py:40
  76.8 5.0 %multiply_reduce_fusion.4 = f32[8,128]{1,0:T(8,128)S(1)} fusion(f32[8,128]{1,0:T(8,128)S(1)} %dynamic-slice_bitcast_fusion.8, f32[8,1024]{1,0:T(8,128)S(1)} %get-tuple-element.419, f32[8,128]{1,0:T(8,128)S(1)} %get-tuple-element.420, f32[8,1024]{1,0:T(8,128)S(1)} %get-tuple-element.421, f32[8,128]{1,0:T(8,128)S(1)} %get-tuple-element.422, ...), kind=kLoop, calls=%fused_computation.7.clone.1 | loop fusion | flops 19921920 | bytes 151552 | tf_op jit(solution)/shard_map/while/body/eval_jaxpr/reduce_sum | solution.py:40
  83.5 5.0 %multiply_reduce_fusion.4 = f32[8,128]{1,0:T(8,128)S(1)} fusion(f32[8,128]{1,0:T(8,128)S(1)} %dynamic-slice_bitcast_fusion.8, f32[8,1024]{1,0:T(8,128)S(1)} %get-tuple-element.419, f32[8,128]{1,0:T(8,128)S(1)} %get-tuple-element.420, f32[8,1024]{1,0:T(8,128)S(1)} %get-tuple-element.421, f32[8,128]{1,0:T(8,128)S(1)} %get-tuple-element.422, ...), kind=kLoop, calls=%fused_computation.7.clone.1 | loop fusion | flops 19921920 | bytes 151552 | tf_op jit(solution)/shard_map/while/body/eval_jaxpr/reduce_sum | solution.py:40
  90.3 5.0 %multiply_reduce_fusion.4 = f32[8,128]{1,0:T(8,128)S(1)} fusion(f32[8,128]{1,0:T(8,128)S(1)} %dynamic-slice_bitcast_fusion.8, f32[8,1024]{1,0:T(8,128)S(1)} %get-tuple-element.419, f32[8,128]{1,0:T(8,128)S(1)} %get-tuple-element.420, f32[8,1024]{1,0:T(8,128)S(1)} %get-tuple-element.421, f32[8,128]{1,0:T(8,128)S(1)} %get-tuple-element.422, ...), kind=kLoop, calls=%fused_computation.7.clone.1 | loop fusion | flops 19921920 | bytes 151552 | tf_op jit(solution)/shard_map/while/body/eval_jaxpr/reduce_sum | solution.py:40
  97.0 5.0 %multiply_reduce_fusion.4 = f32[8,128]{1,0:T(8,128)S(1)} fusion(f32[8,128]{1,0:T(8,128)S(1)} %dynamic-slice_bitcast_fusion.8, f32[8,1024]{1,0:T(8,128)S(1)} %get-tuple-element.419, f32[8,128]{1,0:T(8,128)S(1)} %get-tuple-element.420, f32[8,1024]{1,0:T(8,128)S(1)} %get-tuple-element.421, f32[8,128]{1,0:T(8,128)S(1)} %get-tuple-element.422, ...), kind=kLoop, calls=%fused_computation.7.clone.1 | loop fusion | flops 19921920 | bytes 151552 | tf_op jit(solution)/shard_map/while/body/eval_jaxpr/reduce_sum | solution.py:40
  103.8 5.0 %multiply_reduce_fusion.4 = f32[8,128]{1,0:T(8,128)S(1)} fusion(f32[8,128]{1,0:T(8,128)S(1)} %dynamic-slice_bitcast_fusion.8, f32[8,1024]{1,0:T(8,128)S(1)} %get-tuple-element.419, f32[8,128]{1,0:T(8,128)S(1)} %get-tuple-element.420, f32[8,1024]{1,0:T(8,128)S(1)} %get-tuple-element.421, f32[8,128]{1,0:T(8,128)S(1)} %get-tuple-element.422, ...), kind=kLoop, calls=%fused_computation.7.clone.1 | loop fusion | flops 19921920 | bytes 151552 | tf_op jit(solution)/shard_map/while/body/eval_jaxpr/reduce_sum | solution.py:40
  110.6 5.0 %multiply_reduce_fusion.4 = f32[8,128]{1,0:T(8,128)S(1)} fusion(f32[8,128]{1,0:T(8,128)S(1)} %dynamic-slice_bitcast_fusion.8, f32[8,1024]{1,0:T(8,128)S(1)} %get-tuple-element.419, f32[8,128]{1,0:T(8,128)S(1)} %get-tuple-element.420, f32[8,1024]{1,0:T(8,128)S(1)} %get-tuple-element.421, f32[8,128]{1,0:T(8,128)S(1)} %get-tuple-element.422, ...), kind=kLoop, calls=%fused_computation.7.clone.1 | loop fusion | flops 19921920 | bytes 151552 | tf_op jit(solution)/shard_map/while/body/eval_jaxpr/reduce_sum | solution.py:40
  117.3 5.0 %multiply_reduce_fusion.4 = f32[8,128]{1,0:T(8,128)S(1)} fusion(f32[8,128]{1,0:T(8,128)S(1)} %dynamic-slice_bitcast_fusion.8, f32[8,1024]{1,0:T(8,128)S(1)} %get-tuple-element.419, f32[8,128]{1,0:T(8,128)S(1)} %get-tuple-element.420, f32[8,1024]{1,0:T(8,128)S(1)} %get-tuple-element.421, f32[8,128]{1,0:T(8,128)S(1)} %get-tuple-element.422, ...), kind=kLoop, calls=%fused_computation.7.clone.1 | loop fusion | flops 19921920 | bytes 151552 | tf_op jit(solution)/shard_map/while/body/eval_jaxpr/reduce_sum | solution.py:40
  124.1 5.0 %multiply_reduce_fusion.4 = f32[8,128]{1,0:T(8,128)S(1)} fusion(f32[8,128]{1,0:T(8,128)S(1)} %dynamic-slice_bitcast_fusion.8, f32[8,1024]{1,0:T(8,128)S(1)} %get-tuple-element.419, f32[8,128]{1,0:T(8,128)S(1)} %get-tuple-element.420, f32[8,1024]{1,0:T(8,128)S(1)} %get-tuple-element.421, f32[8,128]{1,0:T(8,128)S(1)} %get-tuple-element.422, ...), kind=kLoop, calls=%fused_computation.7.clone.1 | loop fusion | flops 19921920 | bytes 151552 | tf_op jit(solution)/shard_map/while/body/eval_jaxpr/reduce_sum | solution.py:40
  130.7 1.3 collective-permute-start.3
  132.0 5.4 %collective-permute-start.2 = (f32[5,12,128]{2,0,1:T(8,128)S(1)}, f32[5,12,128]{2,0,1:T(8,128)S(1)}, u32[]{:S(2)}, u32[]{:S(2)}) collective-permute-start(f32[5,12,128]{2,0,1:T(8,128)S(1)} %get-tuple-element.277), channel_id=1, source_target_pairs={{0,4},{4,8},{8,12},{12,16},{16,20},{20,24},{24,28},{1,5},{5,9},{9,... | collective-permute-start | bytes 92168 | tf_op jit(solution)/shard_map/ppermute | solution.py:24
  138.1 3.3 all-to-all-start.1
  144.3 2.2 all-to-all-done.1
  146.8 1.7 concatenate.46
  148.6 1.2 pad_maximum_fusion
  149.8 263.3 %while.27 = (s32[]{:T(128)}, f32[16,3,8,128]{3,2,1,0:T(8,128)S(1)}, f32[16,8,128]{2,1,0:T(8,128)S(1)}, f32[16,8,128]{2,1,0:T(8,128)S(1)}, pred[16,8,1024]{2,1,0:...) while((s32[]{:T(128)}, f32[16,3,8,128]{3,2,1,0:T(8,128)S(1)}, ...), condition=%wide.region_9.10_spmd, body=%wide.region_3.9_spmd.sunk | while | flops 60831936 | bytes 2852473 | solution.py:194
  150.5 0.9 slice_reduce_fusion.19
  152.4 13.7 %multiply_reduce_fusion.5 = (f32[8,128]{1,0:T(8,128)S(1)}, f32[8,128]{1,0:T(8,128)S(1)}, f32[8,128]{1,0:T(8,128)S(1)}, f32[8,128]{1,0:T(8,128)S(1)}, f32[8,128]{1,0:T(8,128)S(1)}) fusion(f32[8,1024]{1,0:T(8,128)S(1)} %bitcast.329, f32[8,128]{1,0:T(8,128)S(1)} %get-tuple-element.434, f32[8,1024]{1,0:T(8,128)S(1)} %bitcast.330, ...), kind=kLoop, calls=%fused_computation.65.clone.1 | loop fusion | flops 60812288 | bytes 430080 | tf_op jit(solution)/shard_map/while/body/eval_jaxpr/reduce_sum | solution.py:78
  167.0 0.9 slice_reduce_fusion.19
  168.9 13.7 %multiply_reduce_fusion.5 = (f32[8,128]{1,0:T(8,128)S(1)}, f32[8,128]{1,0:T(8,128)S(1)}, f32[8,128]{1,0:T(8,128)S(1)}, f32[8,128]{1,0:T(8,128)S(1)}, f32[8,128]{1,0:T(8,128)S(1)}) fusion(f32[8,1024]{1,0:T(8,128)S(1)} %bitcast.329, f32[8,128]{1,0:T(8,128)S(1)} %get-tuple-element.434, f32[8,1024]{1,0:T(8,128)S(1)} %bitcast.330, ...), kind=kLoop, calls=%fused_computation.65.clone.1 | loop fusion | flops 60812288 | bytes 430080 | tf_op jit(solution)/shard_map/while/body/eval_jaxpr/reduce_sum | solution.py:78
  183.4 0.9 slice_reduce_fusion.19
  185.3 13.7 %multiply_reduce_fusion.5 = (f32[8,128]{1,0:T(8,128)S(1)}, f32[8,128]{1,0:T(8,128)S(1)}, f32[8,128]{1,0:T(8,128)S(1)}, f32[8,128]{1,0:T(8,128)S(1)}, f32[8,128]{1,0:T(8,128)S(1)}) fusion(f32[8,1024]{1,0:T(8,128)S(1)} %bitcast.329, f32[8,128]{1,0:T(8,128)S(1)} %get-tuple-element.434, f32[8,1024]{1,0:T(8,128)S(1)} %bitcast.330, ...), kind=kLoop, calls=%fused_computation.65.clone.1 | loop fusion | flops 60812288 | bytes 430080 | tf_op jit(solution)/shard_map/while/body/eval_jaxpr/reduce_sum | solution.py:78
  199.9 0.9 slice_reduce_fusion.19
  201.8 13.7 %multiply_reduce_fusion.5 = (f32[8,128]{1,0:T(8,128)S(1)}, f32[8,128]{1,0:T(8,128)S(1)}, f32[8,128]{1,0:T(8,128)S(1)}, f32[8,128]{1,0:T(8,128)S(1)}, f32[8,128]{1,0:T(8,128)S(1)}) fusion(f32[8,1024]{1,0:T(8,128)S(1)} %bitcast.329, f32[8,128]{1,0:T(8,128)S(1)} %get-tuple-element.434, f32[8,1024]{1,0:T(8,128)S(1)} %bitcast.330, ...), kind=kLoop, calls=%fused_computation.65.clone.1 | loop fusion | flops 60812288 | bytes 430080 | tf_op jit(solution)/shard_map/while/body/eval_jaxpr/reduce_sum | solution.py:78
  216.3 0.9 slice_reduce_fusion.19
  218.3 13.7 %multiply_reduce_fusion.5 = (f32[8,128]{1,0:T(8,128)S(1)}, f32[8,128]{1,0:T(8,128)S(1)}, f32[8,128]{1,0:T(8,128)S(1)}, f32[8,128]{1,0:T(8,128)S(1)}, f32[8,128]{1,0:T(8,128)S(1)}) fusion(f32[8,1024]{1,0:T(8,128)S(1)} %bitcast.329, f32[8,128]{1,0:T(8,128)S(1)} %get-tuple-element.434, f32[8,1024]{1,0:T(8,128)S(1)} %bitcast.330, ...), kind=kLoop, calls=%fused_computation.65.clone.1 | loop fusion | flops 60812288 | bytes 430080 | tf_op jit(solution)/shard_map/while/body/eval_jaxpr/reduce_sum | solution.py:78
  232.8 0.9 slice_reduce_fusion.19
  234.7 13.7 %multiply_reduce_fusion.5 = (f32[8,128]{1,0:T(8,128)S(1)}, f32[8,128]{1,0:T(8,128)S(1)}, f32[8,128]{1,0:T(8,128)S(1)}, f32[8,128]{1,0:T(8,128)S(1)}, f32[8,128]{1,0:T(8,128)S(1)}) fusion(f32[8,1024]{1,0:T(8,128)S(1)} %bitcast.329, f32[8,128]{1,0:T(8,128)S(1)} %get-tuple-element.434, f32[8,1024]{1,0:T(8,128)S(1)} %bitcast.330, ...), kind=kLoop, calls=%fused_computation.65.clone.1 | loop fusion | flops 60812288 | bytes 430080 | tf_op jit(solution)/shard_map/while/body/eval_jaxpr/reduce_sum | solution.py:78
  249.3 0.9 slice_reduce_fusion.19
  251.2 13.7 %multiply_reduce_fusion.5 = (f32[8,128]{1,0:T(8,128)S(1)}, f32[8,128]{1,0:T(8,128)S(1)}, f32[8,128]{1,0:T(8,128)S(1)}, f32[8,128]{1,0:T(8,128)S(1)}, f32[8,128]{1,0:T(8,128)S(1)}) fusion(f32[8,1024]{1,0:T(8,128)S(1)} %bitcast.329, f32[8,128]{1,0:T(8,128)S(1)} %get-tuple-element.434, f32[8,1024]{1,0:T(8,128)S(1)} %bitcast.330, ...), kind=kLoop, calls=%fused_computation.65.clone.1 | loop fusion | flops 60812288 | bytes 430080 | tf_op jit(solution)/shard_map/while/body/eval_jaxpr/reduce_sum | solution.py:78
  265.7 0.9 slice_reduce_fusion.19
  267.6 13.7 %multiply_reduce_fusion.5 = (f32[8,128]{1,0:T(8,128)S(1)}, f32[8,128]{1,0:T(8,128)S(1)}, f32[8,128]{1,0:T(8,128)S(1)}, f32[8,128]{1,0:T(8,128)S(1)}, f32[8,128]{1,0:T(8,128)S(1)}) fusion(f32[8,1024]{1,0:T(8,128)S(1)} %bitcast.329, f32[8,128]{1,0:T(8,128)S(1)} %get-tuple-element.434, f32[8,1024]{1,0:T(8,128)S(1)} %bitcast.330, ...), kind=kLoop, calls=%fused_computation.65.clone.1 | loop fusion | flops 60812288 | bytes 430080 | tf_op jit(solution)/shard_map/while/body/eval_jaxpr/reduce_sum | solution.py:78
  282.2 0.9 slice_reduce_fusion.19
  284.1 13.7 %multiply_reduce_fusion.5 = (f32[8,128]{1,0:T(8,128)S(1)}, f32[8,128]{1,0:T(8,128)S(1)}, f32[8,128]{1,0:T(8,128)S(1)}, f32[8,128]{1,0:T(8,128)S(1)}, f32[8,128]{1,0:T(8,128)S(1)}) fusion(f32[8,1024]{1,0:T(8,128)S(1)} %bitcast.329, f32[8,128]{1,0:T(8,128)S(1)} %get-tuple-element.434, f32[8,1024]{1,0:T(8,128)S(1)} %bitcast.330, ...), kind=kLoop, calls=%fused_computation.65.clone.1 | loop fusion | flops 60812288 | bytes 430080 | tf_op jit(solution)/shard_map/while/body/eval_jaxpr/reduce_sum | solution.py:78
  298.6 0.9 slice_reduce_fusion.19
  300.6 13.7 %multiply_reduce_fusion.5 = (f32[8,128]{1,0:T(8,128)S(1)}, f32[8,128]{1,0:T(8,128)S(1)}, f32[8,128]{1,0:T(8,128)S(1)}, f32[8,128]{1,0:T(8,128)S(1)}, f32[8,128]{1,0:T(8,128)S(1)}) fusion(f32[8,1024]{1,0:T(8,128)S(1)} %bitcast.329, f32[8,128]{1,0:T(8,128)S(1)} %get-tuple-element.434, f32[8,1024]{1,0:T(8,128)S(1)} %bitcast.330, ...), kind=kLoop, calls=%fused_computation.65.clone.1 | loop fusion | flops 60812288 | bytes 430080 | tf_op jit(solution)/shard_map/while/body/eval_jaxpr/reduce_sum | solution.py:78
  315.1 0.9 slice_reduce_fusion.19
  317.0 13.7 %multiply_reduce_fusion.5 = (f32[8,128]{1,0:T(8,128)S(1)}, f32[8,128]{1,0:T(8,128)S(1)}, f32[8,128]{1,0:T(8,128)S(1)}, f32[8,128]{1,0:T(8,128)S(1)}, f32[8,128]{1,0:T(8,128)S(1)}) fusion(f32[8,1024]{1,0:T(8,128)S(1)} %bitcast.329, f32[8,128]{1,0:T(8,128)S(1)} %get-tuple-element.434, f32[8,1024]{1,0:T(8,128)S(1)} %bitcast.330, ...), kind=kLoop, calls=%fused_computation.65.clone.1 | loop fusion | flops 60812288 | bytes 430080 | tf_op jit(solution)/shard_map/while/body/eval_jaxpr/reduce_sum | solution.py:78
  331.6 0.9 slice_reduce_fusion.19
  333.5 13.7 %multiply_reduce_fusion.5 = (f32[8,128]{1,0:T(8,128)S(1)}, f32[8,128]{1,0:T(8,128)S(1)}, f32[8,128]{1,0:T(8,128)S(1)}, f32[8,128]{1,0:T(8,128)S(1)}, f32[8,128]{1,0:T(8,128)S(1)}) fusion(f32[8,1024]{1,0:T(8,128)S(1)} %bitcast.329, f32[8,128]{1,0:T(8,128)S(1)} %get-tuple-element.434, f32[8,1024]{1,0:T(8,128)S(1)} %bitcast.330, ...), kind=kLoop, calls=%fused_computation.65.clone.1 | loop fusion | flops 60812288 | bytes 430080 | tf_op jit(solution)/shard_map/while/body/eval_jaxpr/reduce_sum | solution.py:78
  348.0 0.9 slice_reduce_fusion.19
  349.9 13.7 %multiply_reduce_fusion.5 = (f32[8,128]{1,0:T(8,128)S(1)}, f32[8,128]{1,0:T(8,128)S(1)}, f32[8,128]{1,0:T(8,128)S(1)}, f32[8,128]{1,0:T(8,128)S(1)}, f32[8,128]{1,0:T(8,128)S(1)}) fusion(f32[8,1024]{1,0:T(8,128)S(1)} %bitcast.329, f32[8,128]{1,0:T(8,128)S(1)} %get-tuple-element.434, f32[8,1024]{1,0:T(8,128)S(1)} %bitcast.330, ...), kind=kLoop, calls=%fused_computation.65.clone.1 | loop fusion | flops 60812288 | bytes 430080 | tf_op jit(solution)/shard_map/while/body/eval_jaxpr/reduce_sum | solution.py:78
  364.5 0.9 slice_reduce_fusion.19
  366.4 13.7 %multiply_reduce_fusion.5 = (f32[8,128]{1,0:T(8,128)S(1)}, f32[8,128]{1,0:T(8,128)S(1)}, f32[8,128]{1,0:T(8,128)S(1)}, f32[8,128]{1,0:T(8,128)S(1)}, f32[8,128]{1,0:T(8,128)S(1)}) fusion(f32[8,1024]{1,0:T(8,128)S(1)} %bitcast.329, f32[8,128]{1,0:T(8,128)S(1)} %get-tuple-element.434, f32[8,1024]{1,0:T(8,128)S(1)} %bitcast.330, ...), kind=kLoop, calls=%fused_computation.65.clone.1 | loop fusion | flops 60812288 | bytes 430080 | tf_op jit(solution)/shard_map/while/body/eval_jaxpr/reduce_sum | solution.py:78
  380.9 0.9 slice_reduce_fusion.19
  382.9 13.7 %multiply_reduce_fusion.5 = (f32[8,128]{1,0:T(8,128)S(1)}, f32[8,128]{1,0:T(8,128)S(1)}, f32[8,128]{1,0:T(8,128)S(1)}, f32[8,128]{1,0:T(8,128)S(1)}, f32[8,128]{1,0:T(8,128)S(1)}) fusion(f32[8,1024]{1,0:T(8,128)S(1)} %bitcast.329, f32[8,128]{1,0:T(8,128)S(1)} %get-tuple-element.434, f32[8,1024]{1,0:T(8,128)S(1)} %bitcast.330, ...), kind=kLoop, calls=%fused_computation.65.clone.1 | loop fusion | flops 60812288 | bytes 430080 | tf_op jit(solution)/shard_map/while/body/eval_jaxpr/reduce_sum | solution.py:78
  397.4 0.9 slice_reduce_fusion.19
  399.3 13.7 %multiply_reduce_fusion.5 = (f32[8,128]{1,0:T(8,128)S(1)}, f32[8,128]{1,0:T(8,128)S(1)}, f32[8,128]{1,0:T(8,128)S(1)}, f32[8,128]{1,0:T(8,128)S(1)}, f32[8,128]{1,0:T(8,128)S(1)}) fusion(f32[8,1024]{1,0:T(8,128)S(1)} %bitcast.329, f32[8,128]{1,0:T(8,128)S(1)} %get-tuple-element.434, f32[8,1024]{1,0:T(8,128)S(1)} %bitcast.330, ...), kind=kLoop, calls=%fused_computation.65.clone.1 | loop fusion | flops 60812288 | bytes 430080 | tf_op jit(solution)/shard_map/while/body/eval_jaxpr/reduce_sum | solution.py:78
  413.9 41.0 %pmin.7 = f32[]{:T(128)} all-reduce(f32[]{:T(128)} %fusion.28), channel_id=1, replica_groups=mesh['gx'=8,'gy'=4] {'gx','gy'}, use_global_device_ids=true, to_apply=%region_11.12 | all-reduce | flops 1 | bytes 8 | tf_op jit(solution)/shard_map/pmin | solution.py:202
  454.9 1.4 bitcast_select_fusion.3
  456.9 0.9 bitcast_select_fusion.2
  (628 shorter events, 67.5 us)
Async XLA Ops:
  0.6 16.5 %copy-start.4 = (f32[16384]{0:T(1024)S(1)}, f32[16384]{0:T(1024)}, u32[]{:S(2)}) copy-start(f32[16384]{0:T(1024)} %param.15) | copy-start | bytes 196612
  0.6 15.1 %copy-start = (f32[3,16384]{1,0:T(4,128)S(1)}, f32[3,16384]{1,0:T(4,128)}, u32[]{:S(2)}) copy-start(f32[3,16384]{1,0:T(4,128)} %param.13) | copy-start | bytes 589828
  0.7 15.0 %copy-start.6 = (s32[128]{0:T(128)S(1)}, s32[128]{0:T(128)}, u32[]{:S(2)}) copy-start(s32[128]{0:T(128)} %param.21) | copy-start | bytes 1540
  0.7 15.8 %copy-start.1 = (f32[3,16384]{1,0:T(4,128)S(1)}, f32[3,16384]{1,0:T(4,128)}, u32[]{:S(2)}) copy-start(f32[3,16384]{1,0:T(4,128)} %param.14) | copy-start | bytes 589828
  2.1 15.6 %copy-start.3 = (f32[16384]{0:T(1024)S(1)}, f32[16384]{0:T(1024)}, u32[]{:S(2)}) copy-start(f32[16384]{0:T(1024)} %param.16) | copy-start | bytes 196612
  4.1 15.3 %copy-start.5 = (s32[128,8]{0,1:T(8,128)S(1)}, s32[128,8]{0,1:T(8,128)}, u32[]{:S(2)}) copy-start(s32[128,8]{0,1:T(8,128)} %param.20) | copy-start | bytes 12292
  4.1 16.5 %collective-permute-start.1 = (f32[5,12,128]{2,0,1:T(8,128)S(1)}, f32[5,12,128]{2,0,1:T(8,128)S(1)}, u32[]{:S(2)}, u32[]{:S(2)}) collective-permute-start(f32[5,12,128]{2,0,1:T(8,128)S(1)} %get-tuple-element.280), channel_id=1, source_target_pairs={{4,0},{8,4},{12,8},{16,12},{20,16},{24,20},{28,24},{5,1},{9,5},{13... | collective-permute-start | bytes 92168 | tf_op jit(solution)/shard_map/ppermute | solution.py:25
  5.4 15.2 %collective-permute-start = (f32[5,12,128]{2,0,1:T(8,128)S(1)}, f32[5,12,128]{2,0,1:T(8,128)S(1)}, u32[]{:S(2)}, u32[]{:S(2)}) collective-permute-start(f32[5,12,128]{2,0,1:T(8,128)S(1)} %get-tuple-element.279), channel_id=1, source_target_pairs={{0,4},{4,8},{8,12},{12,16},{16,20},{20,24},{24,28},{1,5},{5,9},{9,... | collective-permute-start | bytes 92168 | tf_op jit(solution)/shard_map/ppermute | solution.py:24
  12.3 8.3 %all-to-all-start = ((f32[5,4,12,128]{3,2,0,1:T(8,128)}), f32[5,4,12,128]{3,2,0,1:T(8,128)S(1)}, u32[]{:S(2)}, u32[]{:S(2)}) async-start(f32[5,4,12,128]{3,2,0,1:T(8,128)} %copy.36), calls=%async_computation | async-start | bytes 327680 | tf_op jit(solution)/shard_map/all_to_all | solution.py:101
  20.9 108.2 %copy-start.2 = (f32[16384]{0:T(1024)S(1)}, f32[16384]{0:T(1024)}, u32[]{:S(2)}) copy-start(f32[16384]{0:T(1024)} %param.17) | copy-start | bytes 196612
  130.7 15.8 %collective-permute-start.3 = (f32[5,12,128]{2,0,1:T(8,128)S(1)}, f32[5,12,128]{2,0,1:T(8,128)S(1)}, u32[]{:S(2)}, u32[]{:S(2)}) collective-permute-start(f32[5,12,128]{2,0,1:T(8,128)S(1)} %get-tuple-element.278), channel_id=1, source_target_pairs={{4,0},{8,4},{12,8},{16,12},{20,16},{24,20},{28,24},{5,1},{9,5},{13... | collective-permute-start | bytes 92168 | tf_op jit(solution)/shard_map/ppermute | solution.py:25
  132.0 14.5 %collective-permute-start.2 = (f32[5,12,128]{2,0,1:T(8,128)S(1)}, f32[5,12,128]{2,0,1:T(8,128)S(1)}, u32[]{:S(2)}, u32[]{:S(2)}) collective-permute-start(f32[5,12,128]{2,0,1:T(8,128)S(1)} %get-tuple-element.277), channel_id=1, source_target_pairs={{0,4},{4,8},{8,12},{12,16},{16,20},{20,24},{24,28},{1,5},{5,9},{9,... | collective-permute-start | bytes 92168 | tf_op jit(solution)/shard_map/ppermute | solution.py:24
  138.1 8.3 %all-to-all-start.1 = ((f32[5,4,12,128]{3,2,0,1:T(8,128)}), f32[5,4,12,128]{3,2,0,1:T(8,128)S(1)}, u32[]{:S(2)}, u32[]{:S(2)}) async-start(f32[5,4,12,128]{3,2,0,1:T(8,128)} %copy.41), calls=%async_computation.1 | async-start | bytes 327680 | tf_op jit(solution)/shard_map/all_to_all | solution.py:140
where the time goes:
time: 459 us; the launch traced here: 458 us
  other arithmetic  309 us (67%)
  local copies, waits for them, and re-layouts  78.7 us (17%)
  blocking collectives  41 us (9%)
  starting transfers between devices  20.2 us (4%)
    reduce_sum x16, other arithmetic, force_sum(): rate = 0.5 * jnp.sum(coef * closing, axis=1)  219 us
    reduce_sum x16, other arithmetic, kernel_sum(): total = jnp.sum(source_weight[:, :, None] * profile, axis=1)  79.5 us
    pmin x1, blocking collectives, shards(): timestep = lax.pmin(local_least, ('gx', 'gy'))  41 us
    slice x16, local copies, waits for them, and re-layouts, force_group(): weight = jnp.where(allowed, source_rows[6], 0.0)  14.8 us
    dynamic_slice x16, local copies, waits for them, and re-layouts, shards(): lax.map(force_group, (grouped_lists, usable_rows, grouped_rows))  12.8 us
    ppermute x2, starting transfers between devices, padded(): before = lax.ppermute(last, axis, up)  10.9 us
    gather x16, local copies, waits for them, and re-layouts, density_group(): source_pos = wide_pos[:, chosen].reshape(3, group, list_width * block_size)  10.5 us
    gather x16, local copies, waits for them, and re-layouts, force_group(): wide_table[:, chosen].reshape(row_count, group, list_width * block_size)  10.1 us
  transfers between devices with their start and end apart: 6, of which 2 were waited for; matrix products, arithmetic and copies ran while one was open for 2% of the time, Pallas kernels for 0%

commit v1 on v0

v1 whole, which is shorter than its diff:
```python
import functools
import math

import jax
import jax.numpy as jnp
from jax import lax
from jax.experimental import pallas as pl
from jax.experimental.pallas import tpu as pltpu
from jax.sharding import PartitionSpec as P

GAMMA = 5.0 / 3.0
COURANT = 0.3
KERNEL_NORM = 21.0 / (16.0 * math.pi)
FORCE_NORM = 160.0 * KERNEL_NORM
FAR_STEP = 1e30
TINY = 1e-30
SURE = 4
ROWS = 8
VMEM_BYTES = 48 * 1024 * 1024
MESH = pl.DeviceIdType.MESH
X, Y, Z, MASS, SMOOTH, VX, VY, VZ, ENERGY, FIELDS = range(10)
RHO, PRESS, SOUND, DERIVED = range(4)


def inverse(value):
    return pltpu.reciprocal(value, approx=True)


def distance(squares):
    return squares * lax.rsqrt(jnp.maximum(squares, TINY))


def on_diagonal(column, first, row):
    lanes = lax.broadcasted_iota(jnp.int32, row.shape, 1)
    sublanes = lax.broadcasted_iota(jnp.int32, row.shape, 0)
    return row + jnp.where(lanes == sublanes + first, column, 0.0)


def for_neighbours(nbr_ref, count_ref, block, width, visit):
    base = block * width
    visit([nbr_ref[base + j] for j in range(SURE)], True)

    def more(j, carry):
        visit([nbr_ref[base + j]], False)
        return carry

    lax.fori_loop(SURE, count_ref[block], more, 0)


def density_kernel(width, nbr_ref, count_ref, live_ref, table_ref, rho_ref, cols, sums):
    size = table_ref.shape[2]
    rho_ref[...] = jnp.zeros_like(rho_ref)

    def target(block, carry):
        own = table_ref[block]
        turned = own.T
        for place, field in enumerate((X, Y, Z)):
            cols[place] = jnp.broadcast_to(turned[:, field : field + 1], (size, size))
        smooth = jnp.broadcast_to(turned[:, SMOOTH : SMOOTH + 1], (size, size))
        cols[3] = 2.0 * smooth
        cols[4] = 2.5 * smooth

        def visit(slots, fresh):
            sources = [
                [table_ref[slot, pl.ds(field, 1), :] for field in (X, Y, Z, MASS)]
                for slot in slots
            ]
            for first in range(0, size, ROWS):
                rows = pl.ds(first, ROWS)
                x, y, z, reach, edge = [cols[place, rows, :] for place in range(5)]
                total = None if fresh else sums[rows, :]
                for sx, sy, sz, mass in sources:
                    dx, dy, dz = x - sx, y - sy, z - sz
                    squares = dx * dx + dy * dy + dz * dz
                    taper = jnp.maximum(reach - distance(squares), 0.0)
                    square = taper * taper
                    term = (square * square) * (mass * (edge - taper))
                    total = term if total is None else total + term
                sums[rows, :] = total

        for_neighbours(nbr_ref, count_ref, block, width, visit)
        row = jnp.zeros((ROWS, size), jnp.float32)
        for first in range(0, size, ROWS):
            row = on_diagonal(
                jnp.sum(sums[pl.ds(first, ROWS), :], axis=1, keepdims=True), first, row
            )
        total = jnp.sum(row, axis=0, keepdims=True)
        smooth = table_ref[block, pl.ds(SMOOTH, 1), :]
        cube = smooth * smooth * smooth
        rho_ref[pl.ds(block, 1), :] = (KERNEL_NORM / 8.0) * total / (cube * cube * smooth * smooth)
        return carry

    lax.fori_loop(0, live_ref[0], target, 0)


def force_kernel(
    width,
    nbr_ref,
    count_ref,
    live_ref,
    table_ref,
    rho_ref,
    accel_ref,
    rate_ref,
    least_ref,
    derived,
    cols,
    sums,
):
    size = table_ref.shape[2]
    slots = table_ref.shape[0]
    accel_ref[...] = jnp.zeros_like(accel_ref)
    rate_ref[...] = jnp.zeros_like(rate_ref)

    def derive(turn, carry):
        start = pl.multiple_of(turn * ROWS, ROWS)
        rho = rho_ref[pl.ds(start, ROWS), :]
        for i in range(ROWS):
            energy = table_ref[start + i, pl.ds(ENERGY, 1), :]
            own = rho[i : i + 1]
            derived[start + i, pl.ds(RHO, 1), :] = own
            derived[start + i, pl.ds(PRESS, 1), :] = (GAMMA - 1.0) * energy / own
            derived[start + i, pl.ds(SOUND, 1), :] = 0.5 * jnp.sqrt(
                GAMMA * (GAMMA - 1.0) * energy
            )
        return carry

    lax.fori_loop(0, slots // ROWS, derive, 0)
    places = [(table_ref, field) for field in (X, Y, Z, VX, VY, VZ, SMOOTH, MASS)]
    places += [(derived, field) for field in (RHO, PRESS, SOUND)]

    def target(block, least):
        turned = table_ref[block].T
        extra = derived[block].T
        count = 0
        for field in (X, Y, Z, VX, VY, VZ, SMOOTH):
            cols[count] = jnp.broadcast_to(turned[:, field : field + 1], (size, size))
            count += 1
        for field in (RHO, PRESS, SOUND):
            cols[count] = jnp.broadcast_to(extra[:, field : field + 1], (size, size))
            count += 1

        def visit(chosen, fresh):
            sources = [
                [ref[slot, pl.ds(field, 1), :] for ref, field in places] for slot in chosen
            ]
            for first in range(0, size, ROWS):
                rows = pl.ds(first, ROWS)
                x, y, z, vx, vy, vz, smooth, dens, press, sound = [
                    cols[place, rows, :] for place in range(10)
                ]
                totals = None if fresh else [sums[i, rows, :] for i in range(5)]
                for sx, sy, sz, svx, svy, svz, ssmooth, mass, sdens, spress, ssound in sources:
                    dx, dy, dz = x - sx, y - sy, z - sz
                    squares = dx * dx + dy * dy + dz * dz
                    closing = dx * (vx - svx) + dy * (vy - svy) + dz * (vz - svz)
                    reach = smooth + ssmooth
                    reach2 = reach * reach
                    reach4 = reach2 * reach2
                    approach = (
                        reach * jnp.minimum(closing, 0.0) * inverse(squares + 0.0025 * reach2)
                    )
                    visc = approach * (approach - (sound + ssound)) * inverse(dens + sdens)
                    taper = jnp.maximum(reach - distance(squares), 0.0)
                    slope = (taper * taper) * (taper * mass) * inverse(reach4 * reach4)
                    coef = (press + spress + visc) * slope
                    terms = [coef * dx, coef * dy, coef * dz, coef * closing]
                    if totals is None:
                        totals = terms + [approach]
                    else:
                        totals = [a + b for a, b in zip(totals, terms)] + [
                            jnp.minimum(totals[4], approach)
                        ]
                for i in range(5):
                    sums[i, rows, :] = totals[i]

        for_neighbours(nbr_ref, count_ref, block, width, visit)
        lines = [jnp.zeros((ROWS, size), jnp.float32) for _ in range(5)]
        for first in range(0, size, ROWS):
            rows = pl.ds(first, ROWS)
            for i in range(5):
                pick = jnp.sum if i < 4 else jnp.min
                lines[i] = on_diagonal(pick(sums[i, rows, :], axis=1, keepdims=True), first, lines[i])
        lines = [jnp.sum(line, axis=0, keepdims=True) for line in lines]
        for i in range(3):
            accel_ref[i, pl.ds(block, 1), :] = FORCE_NORM * lines[i]
        rate_ref[pl.ds(block, 1), :] = (-0.5 * FORCE_NORM) * lines[3]
        signal = -0.5 * lines[4]
        sound = 2.0 * derived[block, pl.ds(SOUND, 1), :]
        smooth = table_ref[block, pl.ds(SMOOTH, 1), :]
        step = COURANT * smooth / (sound + 1.2 * (sound + 2.0 * signal))
        return jnp.minimum(least, step)

    least = lax.fori_loop(0, live_ref[0], target, jnp.full((1, size), FAR_STEP, jnp.float32))
    least_ref[...] = jnp.broadcast_to(jnp.min(least, axis=1, keepdims=True), least_ref.shape)


def least_kernel(axes, local_ref, out_ref, held, *slots_sems):
    barrier = pltpu.get_barrier_semaphore()
    peers = 0
    for axis, count in axes:
        me = lax.axis_index(axis)
        for step in range(1, count):
            pl.semaphore_signal(
                barrier, inc=1, device_id={axis: lax.rem(me + step, count)}, device_id_type=MESH
            )
        peers += count - 1
    pl.semaphore_wait(barrier, peers)
    held[...] = local_ref[...]
    for i, (axis, count) in enumerate(axes):
        slots, send, recv = slots_sems[3 * i : 3 * i + 3]
        me = lax.axis_index(axis)
        copies = []
        for step in range(1, count):
            copy = pltpu.make_async_remote_copy(
                src_ref=held,
                dst_ref=slots.at[step],
                send_sem=send.at[step],
                recv_sem=recv.at[step],
                device_id={axis: lax.rem(me + step, count)},
                device_id_type=MESH,
            )
            copy.start()
            copies.append(copy)
        for copy in copies:
            copy.wait()
        value = held[...]
        for step in range(1, count):
            value = jnp.minimum(value, slots[step])
        held[...] = value
    out_ref[...] = held[...]


def least_of_all(local, axes):
    scratch = [pltpu.VMEM(local.shape, local.dtype)]
    for _, count in axes:
        scratch += [
            pltpu.VMEM((count,) + local.shape, local.dtype),
            pltpu.SemaphoreType.DMA((count,)),
            pltpu.SemaphoreType.DMA((count,)),
        ]
    return pl.pallas_call(
        functools.partial(least_kernel, axes),
        out_shape=jax.ShapeDtypeStruct(local.shape, local.dtype),
        in_specs=[pl.BlockSpec(memory_space=pltpu.VMEM)],
        out_specs=pl.BlockSpec(memory_space=pltpu.VMEM),
        scratch_shapes=scratch,
        compiler_params=pltpu.CompilerParams(collective_id=0, has_side_effects=True),
        name="least_of_all",
    )(local)


def spread(blocks, send_list, peer_count, slot_count):
    size = lax.axis_size("gx")
    up = [(i, i + 1) for i in range(size - 1)]
    down = [(i + 1, i) for i in range(size - 1)]
    to_fine = send_list[0, :peer_count].reshape(-1)
    outgoing = blocks[to_fine].reshape((peer_count, slot_count) + blocks.shape[1:])
    arrived = lax.all_to_all(outgoing, "gy", split_axis=0, concat_axis=0, tiled=True)
    before = lax.ppermute(blocks[send_list[0, peer_count + 1]], "gx", up)
    after = lax.ppermute(blocks[send_list[0, peer_count]], "gx", down)
    return [arrived.reshape((-1,) + blocks.shape[1:]), before, after]


def shards(
    position, velocity, mass, smoothing, energy, live_blocks, send_list, nbr_list, nbr_count
):
    nx, ny = lax.axis_size("gx"), lax.axis_size("gy")
    block_count = nbr_count.shape[0]
    size = mass.shape[0] // block_count
    slot_count = send_list.shape[2]
    width = nbr_list.shape[1]
    cut = lambda array: array.reshape(block_count, size)
    own = jnp.stack(
        [cut(position[i]) for i in range(3)]
        + [cut(mass), cut(smoothing)]
        + [cut(velocity[i]) for i in range(3)]
        + [cut(energy)],
        axis=1,
    )
    table = jnp.concatenate([own] + spread(own, send_list, ny, slot_count), axis=0)
    slots = table.shape[0]
    lists = nbr_list.reshape(-1)
    smem = pl.BlockSpec(memory_space=pltpu.SMEM)
    vmem = pl.BlockSpec(memory_space=pltpu.VMEM)
    params = pltpu.CompilerParams(vmem_limit_bytes=VMEM_BYTES)
    square = jax.ShapeDtypeStruct((block_count, size), jnp.float32)
    rho = pl.pallas_call(
        functools.partial(density_kernel, width),
        out_shape=square,
        in_specs=[smem, smem, smem, vmem],
        out_specs=vmem,
        scratch_shapes=[
            pltpu.VMEM((5, size, size), jnp.float32),
            pltpu.VMEM((size, size), jnp.float32),
        ],
        compiler_params=params,
        name="density",
    )(lists, nbr_count, live_blocks, table)
    wide_rho = jnp.concatenate([rho] + spread(rho, send_list, ny, slot_count), axis=0)
    accel, rate, least = pl.pallas_call(
        functools.partial(force_kernel, width),
        out_shape=[
            jax.ShapeDtypeStruct((3, block_count, size), jnp.float32),
            square,
            jax.ShapeDtypeStruct((8, 128), jnp.float32),
        ],
        in_specs=[smem, smem, smem, vmem, vmem],
        out_specs=[vmem, vmem, vmem],
        scratch_shapes=[
            pltpu.VMEM((slots, 8, size), jnp.float32),
            pltpu.VMEM((10, size, size), jnp.float32),
            pltpu.VMEM((5, size, size), jnp.float32),
        ],
        compiler_params=params,
        name="force",
    )(lists, nbr_count, live_blocks, table, wide_rho)
    timestep = least_of_all(least, (("gy", ny), ("gx", nx)))[0, 0]
    return (rho.reshape(-1), (timestep * accel).reshape(3, -1), (timestep * rate).reshape(-1))


def solution(mesh):
    return jax.shard_map(
        shards,
        mesh=mesh,
        in_specs=(
            P(None, ("gx", "gy")),
            P(None, ("gx", "gy")),
            P(("gx", "gy")),
            P(("gx", "gy")),
            P(("gx", "gy")),
            P(("gx", "gy")),
            P(("gx", "gy"), None, None),
            P(("gx", "gy"), None),
            P(("gx", "gy")),
        ),
        out_specs=(P(("gx", "gy")), P(None, ("gx", "gy")), P(("gx", "gy"))),
        check_vma=False,
    )
```

time: 459 us -> 268 us (0.58)
  other arithmetic: 309 us -> 3.65 us
  Pallas kernels: 0 us -> 189 us
  local copies, waits for them, and re-layouts: 78.7 us -> 15.2 us
  blocking collectives: 41 us -> 0 us
  starting transfers between devices: 20.2 us -> 48.4 us
  waiting for transfers between devices: 3.21 us -> 9.02 us
    reduce_sum x32 -> x0, other arithmetic: 299 us -> none  [the longest x16 219 us: force_sum(): rate = 0.5 * jnp.sum(coef * closing, axis=1)]
    pallas_call x0 -> x3, Pallas kernels: none -> 189 us  [the longest x1 76.7 us: shards(): pl.pallas_call(functools.partial(force_kernel, width), out_shape=[jax.Sha...]
    pmin x1 -> x0, blocking collectives: 41 us -> none  [shards(): timestep = lax.pmin(local_least, ('gx', 'gy'))]
    gather x52 -> x6, local copies, waits for them, and re-layouts: 32.6 us -> 5.94 us  [the longest x2 2.03 us: spread(): blocks[to_fine].reshape((peer_count, slot_count) + blocks.shape[1:])]
    slice x38 -> x2, local copies, waits for them, and re-layouts: 20.4 us -> 1.2 us  [the longest x1 1.18 us: shards(): timestep = least_of_all(least, (('gy', ny), ('gx', nx)))[0, 0]]
    ppermute x4, starting transfers between devices: 13.5 us -> 28.8 us  [the longest x2 26.2 us: spread(): before = lax.ppermute(blocks[send_list[0, peer_count + 1]], 'gx', up)]
    dynamic_slice x32 -> x0, local copies, waits for them, and re-layouts: 13 us -> none  [the longest x16 12.8 us: shards(): lax.map(force_group, (grouped_lists, usable_rows, grouped_rows))]
    all_to_all x2, starting transfers between devices: 6.69 us -> 19.6 us  [spread(): lax.all_to_all(outgoing, 'gy', split_axis=0, concat_axis=0, tiled=True)]
  transfers between devices with their start and end apart: 6 -> 6, of which waited for: 2 -> 3; matrix products, arithmetic and copies ran while one was open for 2% -> 2% of each run, Pallas kernels for 0% -> 0%
where the time goes in v1:
time: 268 us; the launch traced here: 266 us
  Pallas kernels  189 us (71%)
  starting transfers between devices  48.4 us (18%)
  local copies, waits for them, and re-layouts  15.2 us (6%)
  waiting for transfers between devices  9.02 us (3%)
  other arithmetic  3.65 us (1%)
    pallas_call x1, Pallas kernels, shards(): pl.pallas_call(functools.partial(force_kernel, width), out_shape=[jax.Sha...  76.7 us
    pallas_call x1, Pallas kernels, least_of_all(): pl.pallas_call(functools.partial(least_kernel, axes), out_shape=jax.Shape...  73.7 us
    pallas_call x1, Pallas kernels, shards(): pl.pallas_call(functools.partial(density_kernel, width), out_shape=square...  38.2 us
    ppermute x2, starting transfers between devices, spread(): before = lax.ppermute(blocks[send_list[0, peer_count + 1]], 'gx', up)  26.2 us
    all_to_all x2, starting transfers between devices, spread(): lax.all_to_all(outgoing, 'gy', split_axis=0, concat_axis=0, tiled=True)  19.6 us
    ppermute x2, waiting for transfers between devices, spread(): after = lax.ppermute(blocks[send_list[0, peer_count]], 'gx', down)  5.38 us
  transfers between devices with their start and end apart: 6, of which 3 were waited for; matrix products, arithmetic and copies ran while one was open for 2% of the time, Pallas kernels for 0%

profile of v1, /device:TPU:0, one launch (start us, length us, event | category | flops | bytes accessed | tf_op | source)
XLA Modules:
  0.0 266.3 jit_solution(6681490673313724325)
XLA Ops:
  0.6 0.0 copy-start.3
  0.6 0.7 fusion.1
  1.4 1.8 slice_bitcast_fusion
  3.2 2.4 stack.3
  5.6 0.0 copy-start.2
  5.6 0.6 gather_fusion.1
  6.2 4.9 %collective-permute-start = (f32[12,9,128]{2,1,0:T(8,128)S(1)}, f32[12,9,128]{2,1,0:T(8,128)S(1)}, u32[]{:S(2)}, u32[]{:S(2)}) collective-permute-start(f32[12,9,128]{2,1,0:T(8,128)S(1)} %gather_fusion.1), channel_id=1, source_target_pairs={{0,4},{4,8},{8,12},{12,16},{16,20},{20,24},{24,28},{1,5},{5,9},{9,... | collective-permute-start | bytes 165896 | tf_op jit(solution)/shard_map/ppermute | solution.py:260
  11.1 0.0 copy-done.3
  11.1 0.1 reshape_squeeze.4
  11.2 0.6 gather_fusion
  11.8 0.8 copy.14
  12.6 3.5 %all-to-all-start = ((f32[4,12,9,128]{3,1,2,0:T(8,128)}), f32[4,12,9,128]{3,1,2,0:T(8,128)S(1)}, u32[]{:S(2)}, u32[]{:S(2)}) async-start(f32[4,12,9,128]{3,1,2,0:T(8,128)} %copy.14), calls=%async_computation | async-start | bytes 589824 | tf_op jit(solution)/shard_map/all_to_all | solution.py:259
  16.1 0.6 gather_fusion.2
  16.7 1.3 collective-permute-start.1
  18.0 0.0 copy-done.2
  18.0 0.1 copy.13
  18.1 0.1 reshape.114.nbr_ref
  18.8 3.6 %all-to-all-done = f32[4,12,9,128]{3,1,2,0:T(8,128)S(1)} async-done(((f32[4,12,9,128]{3,1,2,0:T(8,128)}), f32[4,12,9,128]{3,1,2,0:T(8,128)S(1)}, u32[]{:S(2)}, u32[]{:S(2)}) %all-to-all-start) | async-done | bytes 221216 | tf_op jit(solution)/shard_map/all_to_all | solution.py:259
  22.4 0.1 copy.15
  22.5 0.0 collective-permute-done
  22.5 1.2 collective-permute-done.1
  23.7 0.0 copy-start.1
  23.7 0.1 pad_maximum_fusion.table_ref
  23.8 0.5 copy-done.1
  24.4 38.2 %density.1 = f32[128,128]{1,0:T(8,128)} custom-call(s32[1024]{0:T(1024)S(1)} %reshape.114.nbr_ref, s32[128]{0:T(128)S(1)} %copy-done.1, s32[1]{0:T(128)S(6)} %copy.19.live_ref, f32[200,9,128]{2,1,0:T(8,128)S(1)} %pad_maximum_fusion.table_ref), custom_call_target="tpu_custom_call" | custom-call | tf_op jit(solution)/shard_map/density/pallas_call | solution.py:288
  62.6 1.4 gather_fusion.3
  64.0 0.6 reshape.118
  64.6 16.2 %all-to-all-start.1 = ((f32[4,12,128]{2,1,0:T(8,128)}), f32[4,12,128]{2,1,0:T(8,128)S(1)}, u32[]{:S(2)}, u32[]{:S(2)}) async-start(f32[4,12,128]{2,1,0:T(8,128)} %reshape.118), calls=%async_computation.1 | async-start | bytes 65536 | tf_op jit(solution)/shard_map/all_to_all | solution.py:259
  80.8 1.4 gather_fusion.4
  82.2 1.4 gather_fusion.5
  83.6 21.4 %collective-permute-start.2 = (f32[12,128]{1,0:T(8,128)S(1)}, f32[12,128]{1,0:T(8,128)S(1)}, u32[]{:S(2)}, u32[]{:S(2)}) collective-permute-start(f32[12,128]{1,0:T(8,128)S(1)} %gather_fusion.4), channel_id=1, source_target_pairs={{0,4},{4,8},{8,12},{12,16},{16,20},{20,24},{24,28},{1,5},{5,9},{9,... | collective-permute-start | bytes 18440 | tf_op jit(solution)/shard_map/ppermute | solution.py:260
  105.0 1.3 collective-permute-start.3
  106.3 0.0 all-to-all-done.1
  106.3 0.0 collective-permute-done.2
  106.3 4.2 %collective-permute-done.3 = f32[12,128]{1,0:T(8,128)S(1)} collective-permute-done((f32[12,128]{1,0:T(8,128)S(1)}, f32[12,128]{1,0:T(8,128)S(1)}, u32[]{:S(2)}, u32[]{:S(2)}) %collective-permute-start.3) | collective-permute-done | bytes 6176 | tf_op jit(solution)/shard_map/ppermute | solution.py:261
  110.5 0.8 pad_maximum_fusion.1.rho_ref
  111.4 76.7 %force.1 = (f32[3,128,128]{2,1,0:T(8,128)S(1)}, f32[128,128]{1,0:T(8,128)S(1)}, f32[8,128]{1,0:T(8,128)S(1)}) custom-call(s32[1024]{0:T(1024)S(1)} %reshape.114.nbr_ref, s32[128]{0:T(128)S(1)} %copy-done.1, s32[1]{0:T(128)S(6)} %copy.19.live_ref, f32[200,9,128]{2,1,0:T(8,128)S(1)} %pad_maximum_fusion.table_ref, f32[200,128]{1,0:T(8,128)S(1)} %pad_maximum_fusion.1.rho_ref), custom_call_target="tpu_custom_call" | custom-call | tf_op jit(solution)/shard_map/force/pallas_call | solution.py:301
  188.0 0.0 copy-start
  188.1 0.6 copy-done
  188.6 73.7 %least_of_all.1 = f32[8,128]{1,0:T(8,128)} custom-call(f32[8,128]{1,0:T(8,128)} %copy-done), custom_call_target="tpu_custom_call" | custom-call | tf_op jit(solution)/shard_map/least_of_all/pallas_call | solution.py:242
  262.3 1.2 slice.42
  263.5 1.3 multiply_bitcast_fusion.1
  264.8 0.7 multiply_bitcast_fusion
  265.4 0.8 copy.18
  (6 shorter events, 0.1 us)
Async XLA Ops:
  0.6 10.5 %copy-start.3 = (s32[1,6,12]{2,0,1:T(1,128)S(1)}, s32[1,6,12]{2,0,1:T(1,128)}, u32[]{:S(2)}) copy-start(s32[1,6,12]{2,0,1:T(1,128)} %param.15) | copy-start | bytes 868
  5.6 12.3 %copy-start.2 = (s32[128,8]{0,1:T(8,128)S(1)}, s32[128,8]{0,1:T(8,128)}, u32[]{:S(2)}) copy-start(s32[128,8]{0,1:T(8,128)} %param.16) | copy-start | bytes 12292
  6.2 16.3 %collective-permute-start = (f32[12,9,128]{2,1,0:T(8,128)S(1)}, f32[12,9,128]{2,1,0:T(8,128)S(1)}, u32[]{:S(2)}, u32[]{:S(2)}) collective-permute-start(f32[12,9,128]{2,1,0:T(8,128)S(1)} %gather_fusion.1), channel_id=1, source_target_pairs={{0,4},{4,8},{8,12},{12,16},{16,20},{20,24},{24,28},{1,5},{5,9},{9,... | collective-permute-start | bytes 165896 | tf_op jit(solution)/shard_map/ppermute | solution.py:260
  12.6 9.8 %all-to-all-start = ((f32[4,12,9,128]{3,1,2,0:T(8,128)}), f32[4,12,9,128]{3,1,2,0:T(8,128)S(1)}, u32[]{:S(2)}, u32[]{:S(2)}) async-start(f32[4,12,9,128]{3,1,2,0:T(8,128)} %copy.14), calls=%async_computation | async-start | bytes 589824 | tf_op jit(solution)/shard_map/all_to_all | solution.py:259
  16.7 7.1 %collective-permute-start.1 = (f32[12,9,128]{2,1,0:T(8,128)S(1)}, f32[12,9,128]{2,1,0:T(8,128)S(1)}, u32[]{:S(2)}, u32[]{:S(2)}) collective-permute-start(f32[12,9,128]{2,1,0:T(8,128)S(1)} %gather_fusion.2), channel_id=1, source_target_pairs={{4,0},{8,4},{12,8},{16,12},{20,16},{24,20},{28,24},{5,1},{9,5},{13... | collective-permute-start | bytes 165896 | tf_op jit(solution)/shard_map/ppermute | solution.py:261
  23.7 0.7 copy-start.1
  64.6 41.6 %all-to-all-start.1 = ((f32[4,12,128]{2,1,0:T(8,128)}), f32[4,12,128]{2,1,0:T(8,128)S(1)}, u32[]{:S(2)}, u32[]{:S(2)}) async-start(f32[4,12,128]{2,1,0:T(8,128)} %reshape.118), calls=%async_computation.1 | async-start | bytes 65536 | tf_op jit(solution)/shard_map/all_to_all | solution.py:259
  83.6 22.7 %collective-permute-start.2 = (f32[12,128]{1,0:T(8,128)S(1)}, f32[12,128]{1,0:T(8,128)S(1)}, u32[]{:S(2)}, u32[]{:S(2)}) collective-permute-start(f32[12,128]{1,0:T(8,128)S(1)} %gather_fusion.4), channel_id=1, source_target_pairs={{0,4},{4,8},{8,12},{12,16},{16,20},{20,24},{24,28},{1,5},{5,9},{9,... | collective-permute-start | bytes 18440 | tf_op jit(solution)/shard_map/ppermute | solution.py:260
  105.0 5.5 %collective-permute-start.3 = (f32[12,128]{1,0:T(8,128)S(1)}, f32[12,128]{1,0:T(8,128)S(1)}, u32[]{:S(2)}, u32[]{:S(2)}) collective-permute-start(f32[12,128]{1,0:T(8,128)S(1)} %gather_fusion.5), channel_id=1, source_target_pairs={{4,0},{8,4},{12,8},{16,12},{20,16},{24,20},{28,24},{5,1},{9,5},{13... | collective-permute-start | bytes 18440 | tf_op jit(solution)/shard_map/ppermute | solution.py:261
  188.0 0.6 copy-start

commit v2 on v1

v2 whole, which is shorter than its diff:
```python
import functools
import math

import jax
import jax.numpy as jnp
from jax import lax
from jax.experimental import pallas as pl
from jax.experimental.pallas import tpu as pltpu
from jax.sharding import PartitionSpec as P

GAMMA = 5.0 / 3.0
COURANT = 0.3
KERNEL_NORM = 21.0 / (16.0 * math.pi)
FORCE_NORM = 160.0 * KERNEL_NORM
FAR_STEP = 1e30
TINY = 1e-30
SURE = 4
ROWS = 8
VMEM_BYTES = 48 * 1024 * 1024
MESH = pl.DeviceIdType.MESH
X, Y, Z, MASS, SMOOTH, VX, VY, VZ, ENERGY = range(9)
RHO, PRESS, SOUND = range(8, 11)
OWN_FIELDS = (X, Y, Z, VX, VY, VZ, SMOOTH, RHO, PRESS, SOUND)


def inverse(value):
    return pltpu.reciprocal(value, approx=True)


def distance(squares):
    return squares * lax.rsqrt(jnp.maximum(squares, TINY))


def on_diagonal(column, first, row):
    lanes = lax.broadcasted_iota(jnp.int32, row.shape, 1)
    sublanes = lax.broadcasted_iota(jnp.int32, row.shape, 0)
    return row + jnp.where(lanes == sublanes + first, column, 0.0)


def sweep(width, nbr_ref, count_ref, live_ref, prepare, first_pass, more_pass):
    live = live_ref[0]
    prepare(0)

    def turn(i, carry):
        block = jnp.minimum(i, live - 1)
        after = jnp.minimum(i + 1, live - 1)
        prior = jnp.maximum(i - 1, 0)
        base = block * width
        count = count_ref[block]
        odd = lax.rem(count - SURE, 2)
        for extra in range(2):

            @pl.when(odd == extra)
            def _():
                first_pass([nbr_ref[base + j] for j in range(SURE + extra)], prior)
                prepare(after)

        done = SURE + odd

        def more(j, carry):
            at = base + done + 2 * j
            more_pass([nbr_ref[at], nbr_ref[at + 1]])
            return carry

        return lax.fori_loop(0, (count - done) // 2, more, carry)

    lax.fori_loop(0, live + 1, turn, 0)


def density_kernel(width, nbr_ref, count_ref, live_ref, table_ref, rho_ref, turned, cols, sums):
    size = table_ref.shape[2]
    rho_ref[...] = jnp.zeros_like(rho_ref)
    chunks = [pl.ds(first, ROWS) for first in range(0, size, ROWS)]

    def prepare(block):
        turned[...] = table_ref[block].T

    def read(slots):
        return [
            [table_ref[slot, pl.ds(field, 1), :] for field in (X, Y, Z, MASS)] for slot in slots
        ]

    def summed(columns, sources, total):
        x, y, z, reach, edge = columns
        for sx, sy, sz, mass in sources:
            dx, dy, dz = x - sx, y - sy, z - sz
            squares = dx * dx + dy * dy + dz * dz
            taper = jnp.maximum(reach - distance(squares), 0.0)
            square = taper * taper
            term = (square * square) * (mass * (edge - taper))
            total = term if total is None else total + term
        return total

    def first_pass(slots, prior):
        sources = read(slots)
        line = jnp.zeros((ROWS, size), jnp.float32)
        for rows in chunks:
            line = on_diagonal(jnp.sum(sums[rows, :], axis=1, keepdims=True), rows.start, line)
            own = turned[rows, :]
            columns = [
                jnp.broadcast_to(own[:, field : field + 1], (ROWS, size))
                for field in (X, Y, Z, SMOOTH)
            ]
            columns[3:] = [2.0 * columns[3], 2.5 * columns[3]]
            for i, column in enumerate(columns):
                cols[i, rows, :] = column
            sums[rows, :] = summed(columns, sources, None)
        total = jnp.sum(line, axis=0, keepdims=True)
        smooth = table_ref[prior, pl.ds(SMOOTH, 1), :]
        cube = smooth * smooth * smooth
        rho_ref[pl.ds(prior, 1), :] = (KERNEL_NORM / 8.0) * total / (cube * cube * smooth * smooth)

    def more_pass(slots):
        sources = read(slots)
        for rows in chunks:
            columns = [cols[i, rows, :] for i in range(5)]
            sums[rows, :] = summed(columns, sources, sums[rows, :])

    sweep(width, nbr_ref, count_ref, live_ref, prepare, first_pass, more_pass)


def force_kernel(
    width,
    nbr_ref,
    count_ref,
    live_ref,
    table_ref,
    rho_ref,
    accel_ref,
    rate_ref,
    least_ref,
    full,
    turned,
    cols,
    sums,
):
    size = table_ref.shape[2]
    slots = table_ref.shape[0]
    accel_ref[...] = jnp.zeros_like(accel_ref)
    rate_ref[...] = jnp.zeros_like(rate_ref)
    least_ref[...] = jnp.full(least_ref.shape, FAR_STEP, jnp.float32)
    chunks = [pl.ds(first, ROWS) for first in range(0, size, ROWS)]

    def derive(turn, carry):
        start = pl.multiple_of(turn * ROWS, ROWS)
        rho = rho_ref[pl.ds(start, ROWS), :]
        for i in range(ROWS):
            slot = start + i
            energy = table_ref[slot, pl.ds(ENERGY, 1), :]
            own = rho[i : i + 1]
            full[slot, pl.ds(0, ENERGY), :] = table_ref[slot, pl.ds(0, ENERGY), :]
            full[slot, pl.ds(RHO, 1), :] = own
            full[slot, pl.ds(PRESS, 1), :] = (GAMMA - 1.0) * energy / own
            full[slot, pl.ds(SOUND, 1), :] = 0.5 * jnp.sqrt(GAMMA * (GAMMA - 1.0) * energy)
        return carry

    lax.fori_loop(0, slots // ROWS, derive, 0)

    def prepare(block):
        turned[...] = full[block].T

    def read(chosen):
        return [
            [full[slot, pl.ds(field, 1), :] for field in OWN_FIELDS + (MASS,)] for slot in chosen
        ]

    def summed(columns, sources, totals):
        x, y, z, vx, vy, vz, smooth, dens, press, sound = columns
        for sx, sy, sz, svx, svy, svz, ssmooth, sdens, spress, ssound, mass in sources:
            dx, dy, dz = x - sx, y - sy, z - sz
            squares = dx * dx + dy * dy + dz * dz
            closing = dx * (vx - svx) + dy * (vy - svy) + dz * (vz - svz)
            reach = smooth + ssmooth
            reach2 = reach * reach
            reach4 = reach2 * reach2
            approach = reach * jnp.minimum(closing, 0.0) * inverse(squares + 0.0025 * reach2)
            visc = approach * (approach - (sound + ssound)) * inverse(dens + sdens)
            taper = jnp.maximum(reach - distance(squares), 0.0)
            slope = (taper * taper) * (taper * mass) * inverse(reach4 * reach4)
            coef = (press + spress + visc) * slope
            terms = [coef * dx, coef * dy, coef * dz, coef * closing]
            if totals is None:
                totals = terms + [approach]
            else:
                totals = [a + b for a, b in zip(totals, terms)] + [
                    jnp.minimum(totals[4], approach)
                ]
        return totals

    def first_pass(chosen, prior):
        sources = read(chosen)
        lines = [jnp.zeros((ROWS, size), jnp.float32) for _ in range(5)]
        for rows in chunks:
            for i in range(5):
                pick = jnp.sum if i < 4 else jnp.min
                lines[i] = on_diagonal(
                    pick(sums[i, rows, :], axis=1, keepdims=True), rows.start, lines[i]
                )
            own = turned[rows, :]
            columns = [
                jnp.broadcast_to(own[:, field : field + 1], (ROWS, size)) for field in OWN_FIELDS
            ]
            for i, column in enumerate(columns):
                cols[i, rows, :] = column
            for i, total in enumerate(summed(columns, sources, None)):
                sums[i, rows, :] = total
        lines = [jnp.sum(line, axis=0, keepdims=True) for line in lines]
        for i in range(3):
            accel_ref[i, pl.ds(prior, 1), :] = FORCE_NORM * lines[i]
        rate_ref[pl.ds(prior, 1), :] = (-0.5 * FORCE_NORM) * lines[3]
        signal = -0.5 * lines[4]
        sound = 2.0 * full[prior, pl.ds(SOUND, 1), :]
        smooth = full[prior, pl.ds(SMOOTH, 1), :]
        step = COURANT * smooth / (sound + 1.2 * (sound + 2.0 * signal))
        least_ref[...] = jnp.minimum(least_ref[...], step)

    def more_pass(chosen):
        sources = read(chosen)
        for rows in chunks:
            columns = [cols[i, rows, :] for i in range(len(OWN_FIELDS))]
            totals = [sums[i, rows, :] for i in range(5)]
            for i, total in enumerate(summed(columns, sources, totals)):
                sums[i, rows, :] = total

    sums[...] = jnp.zeros_like(sums)
    sweep(width, nbr_ref, count_ref, live_ref, prepare, first_pass, more_pass)
    least = jnp.min(least_ref[...], axis=1, keepdims=True)
    least_ref[...] = jnp.broadcast_to(least, least_ref.shape)


def least_kernel(axes, local_ref, out_ref, held, *slots_sems):
    barrier = pltpu.get_barrier_semaphore()
    peers = 0
    for axis, count in axes:
        me = lax.axis_index(axis)
        for step in range(1, count):
            pl.semaphore_signal(
                barrier, inc=1, device_id={axis: lax.rem(me + step, count)}, device_id_type=MESH
            )
        peers += count - 1
    pl.semaphore_wait(barrier, peers)
    held[...] = local_ref[...]
    for i, (axis, count) in enumerate(axes):
        slots, send, recv = slots_sems[3 * i : 3 * i + 3]
        me = lax.axis_index(axis)
        copies = []
        for step in range(1, count):
            copy = pltpu.make_async_remote_copy(
                src_ref=held,
                dst_ref=slots.at[step],
                send_sem=send.at[step],
                recv_sem=recv.at[step],
                device_id={axis: lax.rem(me + step, count)},
                device_id_type=MESH,
            )
            copy.start()
            copies.append(copy)
        for copy in copies:
            copy.wait()
        value = held[...]
        for step in range(1, count):
            value = jnp.minimum(value, slots[step])
        held[...] = value
    out_ref[...] = held[...]


def least_of_all(local, axes):
    scratch = [pltpu.VMEM(local.shape, local.dtype)]
    for _, count in axes:
        scratch += [
            pltpu.VMEM((count,) + local.shape, local.dtype),
            pltpu.SemaphoreType.DMA((count,)),
            pltpu.SemaphoreType.DMA((count,)),
        ]
    return pl.pallas_call(
        functools.partial(least_kernel, axes),
        out_shape=jax.ShapeDtypeStruct(local.shape, local.dtype),
        in_specs=[pl.BlockSpec(memory_space=pltpu.VMEM)],
        out_specs=pl.BlockSpec(memory_space=pltpu.VMEM),
        scratch_shapes=scratch,
        compiler_params=pltpu.CompilerParams(collective_id=0, has_side_effects=True),
        name="least_of_all",
    )(local)


def spread(blocks, send_list, peer_count, slot_count):
    size = lax.axis_size("gx")
    up = [(i, i + 1) for i in range(size - 1)]
    down = [(i + 1, i) for i in range(size - 1)]
    to_fine = send_list[0, :peer_count].reshape(-1)
    outgoing = blocks[to_fine].reshape((peer_count, slot_count) + blocks.shape[1:])
    arrived = lax.all_to_all(outgoing, "gy", split_axis=0, concat_axis=0, tiled=True)
    before = lax.ppermute(blocks[send_list[0, peer_count + 1]], "gx", up)
    after = lax.ppermute(blocks[send_list[0, peer_count]], "gx", down)
    return [arrived.reshape((-1,) + blocks.shape[1:]), before, after]


def shards(
    position, velocity, mass, smoothing, energy, live_blocks, send_list, nbr_list, nbr_count
):
    nx, ny = lax.axis_size("gx"), lax.axis_size("gy")
    block_count = nbr_count.shape[0]
    size = mass.shape[0] // block_count
    slot_count = send_list.shape[2]
    width = nbr_list.shape[1]
    cut = lambda array: array.reshape(block_count, size)
    own = jnp.stack(
        [cut(position[i]) for i in range(3)]
        + [cut(mass), cut(smoothing)]
        + [cut(velocity[i]) for i in range(3)]
        + [cut(energy)],
        axis=1,
    )
    table = jnp.concatenate([own] + spread(own, send_list, ny, slot_count), axis=0)
    slots = table.shape[0]
    lists = nbr_list.reshape(-1)
    smem = pl.BlockSpec(memory_space=pltpu.SMEM)
    vmem = pl.BlockSpec(memory_space=pltpu.VMEM)
    params = pltpu.CompilerParams(vmem_limit_bytes=VMEM_BYTES)
    square = jax.ShapeDtypeStruct((block_count, size), jnp.float32)
    rho = pl.pallas_call(
        functools.partial(density_kernel, width),
        out_shape=square,
        in_specs=[smem, smem, smem, vmem],
        out_specs=vmem,
        scratch_shapes=[
            pltpu.VMEM((size, table.shape[1]), jnp.float32),
            pltpu.VMEM((5, size, size), jnp.float32),
            pltpu.VMEM((size, size), jnp.float32),
        ],
        compiler_params=params,
        name="density",
    )(lists, nbr_count, live_blocks, table)
    wide_rho = jnp.concatenate([rho] + spread(rho, send_list, ny, slot_count), axis=0)
    accel, rate, least = pl.pallas_call(
        functools.partial(force_kernel, width),
        out_shape=[
            jax.ShapeDtypeStruct((3, block_count, size), jnp.float32),
            square,
            jax.ShapeDtypeStruct((8, 128), jnp.float32),
        ],
        in_specs=[smem, smem, smem, vmem, vmem],
        out_specs=[vmem, vmem, vmem],
        scratch_shapes=[
            pltpu.VMEM((slots, 16, size), jnp.float32),
            pltpu.VMEM((size, 16), jnp.float32),
            pltpu.VMEM((len(OWN_FIELDS), size, size), jnp.float32),
            pltpu.VMEM((5, size, size), jnp.float32),
        ],
        compiler_params=params,
        name="force",
    )(lists, nbr_count, live_blocks, table, wide_rho)
    timestep = least_of_all(least, (("gy", ny), ("gx", nx)))[0, 0]
    return (rho.reshape(-1), (timestep * accel).reshape(3, -1), (timestep * rate).reshape(-1))


def solution(mesh):
    return jax.shard_map(
        shards,
        mesh=mesh,
        in_specs=(
            P(None, ("gx", "gy")),
            P(None, ("gx", "gy")),
            P(("gx", "gy")),
            P(("gx", "gy")),
            P(("gx", "gy")),
            P(("gx", "gy")),
            P(("gx", "gy"), None, None),
            P(("gx", "gy"), None),
            P(("gx", "gy")),
        ),
        out_specs=(P(("gx", "gy")), P(None, ("gx", "gy")), P(("gx", "gy"))),
        check_vma=False,
    )
```

time: 268 us -> 267 us (level)
  starting transfers between devices: 48.4 us -> 20.2 us
  Pallas kernels: 189 us -> 216 us
    pallas_call x1, Pallas kernels: 76.7 us -> 136 us  [shards(): pl.pallas_call(functools.partial(force_kernel, width), out_shape=[jax.Sha...]
    pallas_call x1, Pallas kernels: 73.7 us -> 29.3 us  [least_of_all(): pl.pallas_call(functools.partial(least_kernel, axes), out_shape=jax.Shape...]
    ppermute x2, starting transfers between devices: 26.2 us -> 10.9 us  [spread(): before = lax.ppermute(blocks[send_list[0, peer_count + 1]], 'gx', up)]
    all_to_all x2, starting transfers between devices: 19.6 us -> 6.71 us  [spread(): lax.all_to_all(outgoing, 'gy', split_axis=0, concat_axis=0, tiled=True)]
    pallas_call x1, Pallas kernels: 38.2 us -> 50.8 us  [shards(): pl.pallas_call(functools.partial(density_kernel, width), out_shape=square...]
where the time goes in v2:
time: 267 us; the launch traced here: 266 us
  Pallas kernels  216 us (81%)
  starting transfers between devices  20.2 us (8%)
  local copies, waits for them, and re-layouts  15.2 us (6%)
  waiting for transfers between devices  9.02 us (3%)
  other arithmetic  3.65 us (1%)
    pallas_call x1, Pallas kernels, shards(): pl.pallas_call(functools.partial(force_kernel, width), out_shape=[jax.Sha...  136 us
    pallas_call x1, Pallas kernels, shards(): pl.pallas_call(functools.partial(density_kernel, width), out_shape=square...  50.8 us
    pallas_call x1, Pallas kernels, least_of_all(): pl.pallas_call(functools.partial(least_kernel, axes), out_shape=jax.Shape...  29.3 us
    ppermute x2, starting transfers between devices, spread(): before = lax.ppermute(blocks[send_list[0, peer_count + 1]], 'gx', up)  10.9 us
    all_to_all x2, starting transfers between devices, spread(): lax.all_to_all(outgoing, 'gy', split_axis=0, concat_axis=0, tiled=True)  6.71 us
    ppermute x2, waiting for transfers between devices, spread(): after = lax.ppermute(blocks[send_list[0, peer_count]], 'gx', down)  5.38 us
  transfers between devices with their start and end apart: 6, of which 3 were waited for; matrix products, arithmetic and copies ran while one was open for 2% of the time, Pallas kernels for 0%

profile of v2, /device:TPU:0, one launch (start us, length us, event | category | flops | bytes accessed | tf_op | source)
XLA Modules:
  0.0 265.7 jit_solution(14220381522689351944)
XLA Ops:
  0.6 0.0 copy-start.3
  0.6 0.7 fusion.1
  1.4 1.8 slice_bitcast_fusion
  3.2 2.4 stack.3
  5.6 0.0 copy-start.2
  5.6 0.6 gather_fusion.1
  6.2 4.9 %collective-permute-start = (f32[12,9,128]{2,1,0:T(8,128)S(1)}, f32[12,9,128]{2,1,0:T(8,128)S(1)}, u32[]{:S(2)}, u32[]{:S(2)}) collective-permute-start(f32[12,9,128]{2,1,0:T(8,128)S(1)} %gather_fusion.1), channel_id=1, source_target_pairs={{0,4},{4,8},{8,12},{12,16},{16,20},{20,24},{24,28},{1,5},{5,9},{9,... | collective-permute-start | bytes 165896 | tf_op jit(solution)/shard_map/ppermute | solution.py:293
  11.1 0.0 copy-done.3
  11.1 0.1 reshape_squeeze.4
  11.2 0.6 gather_fusion
  11.8 0.8 copy.14
  12.6 3.5 %all-to-all-start = ((f32[4,12,9,128]{3,1,2,0:T(8,128)}), f32[4,12,9,128]{3,1,2,0:T(8,128)S(1)}, u32[]{:S(2)}, u32[]{:S(2)}) async-start(f32[4,12,9,128]{3,1,2,0:T(8,128)} %copy.14), calls=%async_computation | async-start | bytes 589824 | tf_op jit(solution)/shard_map/all_to_all | solution.py:292
  16.1 0.6 gather_fusion.2
  16.7 1.3 collective-permute-start.1
  18.0 0.0 copy-done.2
  18.0 0.1 copy.13
  18.1 0.1 reshape.114.nbr_ref
  18.8 3.6 %all-to-all-done = f32[4,12,9,128]{3,1,2,0:T(8,128)S(1)} async-done(((f32[4,12,9,128]{3,1,2,0:T(8,128)}), f32[4,12,9,128]{3,1,2,0:T(8,128)S(1)}, u32[]{:S(2)}, u32[]{:S(2)}) %all-to-all-start) | async-done | bytes 221216 | tf_op jit(solution)/shard_map/all_to_all | solution.py:292
  22.4 0.1 copy.15
  22.5 0.0 collective-permute-done
  22.5 1.2 collective-permute-done.1
  23.7 0.0 copy-start.1
  23.7 0.1 pad_maximum_fusion.table_ref
  23.8 0.5 copy-done.1
  24.4 50.8 %density.1 = f32[128,128]{1,0:T(8,128)} custom-call(s32[1024]{0:T(1024)S(1)} %reshape.114.nbr_ref, s32[128]{0:T(128)S(1)} %copy-done.1, s32[1]{0:T(128)S(6)} %copy.19.live_ref, f32[200,9,128]{2,1,0:T(8,128)S(1)} %pad_maximum_fusion.table_ref), custom_call_target="tpu_custom_call" | custom-call | tf_op jit(solution)/shard_map/density/pallas_call | solution.py:321
  75.1 1.4 gather_fusion.3
  76.6 0.6 reshape.118
  77.2 3.3 %all-to-all-start.1 = ((f32[4,12,128]{2,1,0:T(8,128)}), f32[4,12,128]{2,1,0:T(8,128)S(1)}, u32[]{:S(2)}, u32[]{:S(2)}) async-start(f32[4,12,128]{2,1,0:T(8,128)} %reshape.118), calls=%async_computation.1 | async-start | bytes 65536 | tf_op jit(solution)/shard_map/all_to_all | solution.py:292
  80.5 1.4 gather_fusion.4
  81.9 1.4 gather_fusion.5
  83.3 6.0 %collective-permute-start.2 = (f32[12,128]{1,0:T(8,128)S(1)}, f32[12,128]{1,0:T(8,128)S(1)}, u32[]{:S(2)}, u32[]{:S(2)}) collective-permute-start(f32[12,128]{1,0:T(8,128)S(1)} %gather_fusion.4), channel_id=1, source_target_pairs={{0,4},{4,8},{8,12},{12,16},{16,20},{20,24},{24,28},{1,5},{5,9},{9,... | collective-permute-start | bytes 18440 | tf_op jit(solution)/shard_map/ppermute | solution.py:293
  89.3 1.3 collective-permute-start.3
  90.6 0.0 all-to-all-done.1
  90.6 0.0 collective-permute-done.2
  90.6 4.2 %collective-permute-done.3 = f32[12,128]{1,0:T(8,128)S(1)} collective-permute-done((f32[12,128]{1,0:T(8,128)S(1)}, f32[12,128]{1,0:T(8,128)S(1)}, u32[]{:S(2)}, u32[]{:S(2)}) %collective-permute-start.3) | collective-permute-done | bytes 6176 | tf_op jit(solution)/shard_map/ppermute | solution.py:294
  94.8 0.8 pad_maximum_fusion.1.rho_ref
  95.7 136.2 %force.1 = (f32[3,128,128]{2,1,0:T(8,128)S(1)}, f32[128,128]{1,0:T(8,128)S(1)}, f32[8,128]{1,0:T(8,128)S(1)}) custom-call(s32[1024]{0:T(1024)S(1)} %reshape.114.nbr_ref, s32[128]{0:T(128)S(1)} %copy-done.1, s32[1]{0:T(128)S(6)} %copy.19.live_ref, f32[200,9,128]{2,1,0:T(8,128)S(1)} %pad_maximum_fusion.table_ref, f32[200,128]{1,0:T(8,128)S(1)} %pad_maximum_fusion.1.rho_ref), custom_call_target="tpu_custom_call" | custom-call | tf_op jit(solution)/shard_map/force/pallas_call | solution.py:335
  231.9 0.0 copy-start
  231.9 0.6 copy-done
  232.5 29.3 %least_of_all.1 = f32[8,128]{1,0:T(8,128)} custom-call(f32[8,128]{1,0:T(8,128)} %copy-done), custom_call_target="tpu_custom_call" | custom-call | tf_op jit(solution)/shard_map/least_of_all/pallas_call | solution.py:275
  261.7 1.2 slice.42
  262.9 1.3 multiply_bitcast_fusion.1
  264.2 0.7 multiply_bitcast_fusion
  264.9 0.8 copy.18
  (6 shorter events, 0.1 us)
Async XLA Ops:
  0.6 10.5 %copy-start.3 = (s32[1,6,12]{2,0,1:T(1,128)S(1)}, s32[1,6,12]{2,0,1:T(1,128)}, u32[]{:S(2)}) copy-start(s32[1,6,12]{2,0,1:T(1,128)} %param.15) | copy-start | bytes 868
  5.6 12.3 %copy-start.2 = (s32[128,8]{0,1:T(8,128)S(1)}, s32[128,8]{0,1:T(8,128)}, u32[]{:S(2)}) copy-start(s32[128,8]{0,1:T(8,128)} %param.16) | copy-start | bytes 12292
  6.2 16.3 %collective-permute-start = (f32[12,9,128]{2,1,0:T(8,128)S(1)}, f32[12,9,128]{2,1,0:T(8,128)S(1)}, u32[]{:S(2)}, u32[]{:S(2)}) collective-permute-start(f32[12,9,128]{2,1,0:T(8,128)S(1)} %gather_fusion.1), channel_id=1, source_target_pairs={{0,4},{4,8},{8,12},{12,16},{16,20},{20,24},{24,28},{1,5},{5,9},{9,... | collective-permute-start | bytes 165896 | tf_op jit(solution)/shard_map/ppermute | solution.py:293
  12.6 9.8 %all-to-all-start = ((f32[4,12,9,128]{3,1,2,0:T(8,128)}), f32[4,12,9,128]{3,1,2,0:T(8,128)S(1)}, u32[]{:S(2)}, u32[]{:S(2)}) async-start(f32[4,12,9,128]{3,1,2,0:T(8,128)} %copy.14), calls=%async_computation | async-start | bytes 589824 | tf_op jit(solution)/shard_map/all_to_all | solution.py:292
  16.7 7.1 %collective-permute-start.1 = (f32[12,9,128]{2,1,0:T(8,128)S(1)}, f32[12,9,128]{2,1,0:T(8,128)S(1)}, u32[]{:S(2)}, u32[]{:S(2)}) collective-permute-start(f32[12,9,128]{2,1,0:T(8,128)S(1)} %gather_fusion.2), channel_id=1, source_target_pairs={{4,0},{8,4},{12,8},{16,12},{20,16},{24,20},{28,24},{5,1},{9,5},{13... | collective-permute-start | bytes 165896 | tf_op jit(solution)/shard_map/ppermute | solution.py:294
  23.7 0.7 copy-start.1
  77.2 13.4 %all-to-all-start.1 = ((f32[4,12,128]{2,1,0:T(8,128)}), f32[4,12,128]{2,1,0:T(8,128)S(1)}, u32[]{:S(2)}, u32[]{:S(2)}) async-start(f32[4,12,128]{2,1,0:T(8,128)} %reshape.118), calls=%async_computation.1 | async-start | bytes 65536 | tf_op jit(solution)/shard_map/all_to_all | solution.py:292
  83.3 7.4 %collective-permute-start.2 = (f32[12,128]{1,0:T(8,128)S(1)}, f32[12,128]{1,0:T(8,128)S(1)}, u32[]{:S(2)}, u32[]{:S(2)}) collective-permute-start(f32[12,128]{1,0:T(8,128)S(1)} %gather_fusion.4), channel_id=1, source_target_pairs={{0,4},{4,8},{8,12},{12,16},{16,20},{20,24},{24,28},{1,5},{5,9},{9,... | collective-permute-start | bytes 18440 | tf_op jit(solution)/shard_map/ppermute | solution.py:293
  89.3 5.5 %collective-permute-start.3 = (f32[12,128]{1,0:T(8,128)S(1)}, f32[12,128]{1,0:T(8,128)S(1)}, u32[]{:S(2)}, u32[]{:S(2)}) collective-permute-start(f32[12,128]{1,0:T(8,128)S(1)} %gather_fusion.5), channel_id=1, source_target_pairs={{4,0},{8,4},{12,8},{16,12},{20,16},{24,20},{28,24},{5,1},{9,5},{13... | collective-permute-start | bytes 18440 | tf_op jit(solution)/shard_map/ppermute | solution.py:294
  231.9 0.6 copy-start

commit v3 on v2

--- a/solution.py
+++ b/solution.py
@@ -67,54 +67,71 @@
     lax.fori_loop(0, live + 1, turn, 0)
 
 
-def density_kernel(width, nbr_ref, count_ref, live_ref, table_ref, rho_ref, turned, cols, sums):
+def grouped(size, count):
+    chunks = [pl.ds(first, ROWS) for first in range(0, size, ROWS)]
+    return [chunks[i : i + count] for i in range(0, len(chunks), count)]
+
+
+def density_kernel(
+    width, nbr_ref, count_ref, live_ref, table_ref, rho_ref, wide, turned, cols, sums
+):
     size = table_ref.shape[2]
     rho_ref[...] = jnp.zeros_like(rho_ref)
-    chunks = [pl.ds(first, ROWS) for first in range(0, size, ROWS)]
+
+    def widen(slot, carry):
+        for i, field in enumerate((X, Y, Z, MASS)):
+            wide[slot, i] = jnp.broadcast_to(table_ref[slot, pl.ds(field, 1), :], (ROWS, size))
+        return carry
+
+    lax.fori_loop(0, table_ref.shape[0], widen, 0)
 
     def prepare(block):
         turned[...] = table_ref[block].T
 
-    def read(slots):
-        return [
-            [table_ref[slot, pl.ds(field, 1), :] for field in (X, Y, Z, MASS)] for slot in slots
-        ]
-
-    def summed(columns, sources, total):
+    def term(columns, source):
         x, y, z, reach, edge = columns
-        for sx, sy, sz, mass in sources:
-            dx, dy, dz = x - sx, y - sy, z - sz
-            squares = dx * dx + dy * dy + dz * dz
-            taper = jnp.maximum(reach - distance(squares), 0.0)
-            square = taper * taper
-            term = (square * square) * (mass * (edge - taper))
-            total = term if total is None else total + term
-        return total
+        sx, sy, sz, mass = source
+        dx, dy, dz = x - sx, y - sy, z - sz
+        squares = dx * dx + dy * dy + dz * dz
+        taper = jnp.maximum(reach - distance(squares), 0.0)
+        square = taper * taper
+        return (square * square) * (mass * (edge - taper))
+
+    def summed(columns, slots, totals):
+        for slot in slots:
+            source = [wide[slot, i] for i in range(4)]
+            terms = [term(own, source) for own in columns]
+            totals = terms if totals is None else [a + b for a, b in zip(totals, terms)]
+        return totals
 
     def first_pass(slots, prior):
-        sources = read(slots)
         line = jnp.zeros((ROWS, size), jnp.float32)
-        for rows in chunks:
-            line = on_diagonal(jnp.sum(sums[rows, :], axis=1, keepdims=True), rows.start, line)
-            own = turned[rows, :]
-            columns = [
-                jnp.broadcast_to(own[:, field : field + 1], (ROWS, size))
-                for field in (X, Y, Z, SMOOTH)
-            ]
-            columns[3:] = [2.0 * columns[3], 2.5 * columns[3]]
-            for i, column in enumerate(columns):
-                cols[i, rows, :] = column
-            sums[rows, :] = summed(columns, sources, None)
+        for group in grouped(size, 4):
+            columns = []
+            for rows in group:
+                line = on_diagonal(jnp.sum(sums[rows, :], axis=1, keepdims=True), rows.start, line)
+                own = turned[rows, :]
+                parts = [
+                    jnp.broadcast_to(own[:, field : field + 1], (ROWS, size))
+                    for field in (X, Y, Z, SMOOTH)
+                ]
+                parts[3:] = [2.0 * parts[3], 2.5 * parts[3]]
+                for i, part in enumerate(parts):
+                    cols[i, rows, :] = part
+                columns.append(parts)
+            for rows, total in zip(group, summed(columns, slots, None)):
+                sums[rows, :] = total
         total = jnp.sum(line, axis=0, keepdims=True)
         smooth = table_ref[prior, pl.ds(SMOOTH, 1), :]
         cube = smooth * smooth * smooth
         rho_ref[pl.ds(prior, 1), :] = (KERNEL_NORM / 8.0) * total / (cube * cube * smooth * smooth)
 
     def more_pass(slots):
-        sources = read(slots)
-        for rows in chunks:
-            columns = [cols[i, rows, :] for i in range(5)]
-            sums[rows, :] = summed(columns, sources, sums[rows, :])
+        for group in grouped(size, 4):
+            columns = [[cols[i, rows, :] for i in range(5)] for rows in group]
+            totals = [sums[rows, :] for rows in group]
+            for rows, total in zip(group, summed(columns, slots, totals)):
+                sums[rows, :] = total
 
     sweep(width, nbr_ref, count_ref, live_ref, prepare, first_pass, more_pass)
 
@@ -130,6 +147,7 @@
     rate_ref,
     least_ref,
     full,
+    wide,
     turned,
     cols,
     sums,
@@ -139,7 +157,6 @@
     accel_ref[...] = jnp.zeros_like(accel_ref)
     rate_ref[...] = jnp.zeros_like(rate_ref)
     least_ref[...] = jnp.full(least_ref.shape, FAR_STEP, jnp.float32)
-    chunks = [pl.ds(first, ROWS) for first in range(0, size, ROWS)]
 
     def derive(turn, carry):
         start = pl.multiple_of(turn * ROWS, ROWS)
@@ -152,6 +169,8 @@
             full[slot, pl.ds(RHO, 1), :] = own
             full[slot, pl.ds(PRESS, 1), :] = (GAMMA - 1.0) * energy / own
             full[slot, pl.ds(SOUND, 1), :] = 0.5 * jnp.sqrt(GAMMA * (GAMMA - 1.0) * energy)
+            for j, field in enumerate(OWN_FIELDS + (MASS,)):
+                wide[slot, j] = jnp.broadcast_to(full[slot, pl.ds(field, 1), :], (ROWS, size))
         return carry
 
     lax.fori_loop(0, slots // ROWS, derive, 0)
@@ -159,51 +178,53 @@
     def prepare(block):
         turned[...] = full[block].T
 
-    def read(chosen):
-        return [
-            [full[slot, pl.ds(field, 1), :] for field in OWN_FIELDS + (MASS,)] for slot in chosen
-        ]
-
-    def summed(columns, sources, totals):
+    def terms(columns, source):
         x, y, z, vx, vy, vz, smooth, dens, press, sound = columns
-        for sx, sy, sz, svx, svy, svz, ssmooth, sdens, spress, ssound, mass in sources:
-            dx, dy, dz = x - sx, y - sy, z - sz
-            squares = dx * dx + dy * dy + dz * dz
-            closing = dx * (vx - svx) + dy * (vy - svy) + dz * (vz - svz)
-            reach = smooth + ssmooth
-            reach2 = reach * reach
-            reach4 = reach2 * reach2
-            approach = reach * jnp.minimum(closing, 0.0) * inverse(squares + 0.0025 * reach2)
-            visc = approach * (approach - (sound + ssound)) * inverse(dens + sdens)
-            taper = jnp.maximum(reach - distance(squares), 0.0)
-            slope = (taper * taper) * (taper * mass) * inverse(reach4 * reach4)
-            coef = (press + spress + visc) * slope
-            terms = [coef * dx, coef * dy, coef * dz, coef * closing]
-            if totals is None:
-                totals = terms + [approach]
-            else:
-                totals = [a + b for a, b in zip(totals, terms)] + [
-                    jnp.minimum(totals[4], approach)
+        sx, sy, sz, svx, svy, svz, ssmooth, sdens, spress, ssound, mass = source
+        dx, dy, dz = x - sx, y - sy, z - sz
+        squares = dx * dx + dy * dy + dz * dz
+        closing = dx * (vx - svx) + dy * (vy - svy) + dz * (vz - svz)
+        reach = smooth + ssmooth
+        reach2 = reach * reach
+        reach4 = reach2 * reach2
+        approach = reach * jnp.minimum(closing, 0.0) * inverse(squares + 0.0025 * reach2)
+        visc = approach * (approach - (sound + ssound)) * inverse(dens + sdens)
+        taper = jnp.maximum(reach - distance(squares), 0.0)
+        slope = (taper * taper) * (taper * mass) * inverse(reach4 * reach4)
+        coef = (press + spress + visc) * slope
+        return [coef * dx, coef * dy, coef * dz, coef * closing, approach]
+
+    def joined(totals, more):
+        return [a + b for a, b in zip(totals[:4], more)] + [jnp.minimum(totals[4], more[4])]
+
+    def summed(columns, chosen, totals):
+        for slot in chosen:
+            source = [wide[slot, j] for j in range(len(OWN_FIELDS) + 1)]
+            more = [terms(own, source) for own in columns]
+            totals = more if totals is None else [joined(*both) for both in zip(totals, more)]
+        return totals
+
+    def first_pass(chosen, prior):
+        lines = [jnp.zeros((ROWS, size), jnp.float32) for _ in range(5)]
+        for group in grouped(size, 2):
+            columns = []
+            for rows in group:
+                for i in range(5):
+                    pick = jnp.sum if i < 4 else jnp.min
+                    lines[i] = on_diagonal(
+                        pick(sums[i, rows, :], axis=1, keepdims=True), rows.start, lines[i]
+                    )
+                own = turned[rows, :]
+                parts = [
+                    jnp.broadcast_to(own[:, field : field + 1], (ROWS, size))
+                    for field in OWN_FIELDS
                 ]
-        return totals
-
-    def first_pass(chosen, prior):
-        sources = read(chosen)
-        lines = [jnp.zeros((ROWS, size), jnp.float32) for _ in range(5)]
-        for rows in chunks:
-            for i in range(5):
-                pick = jnp.sum if i < 4 else jnp.min
-                lines[i] = on_diagonal(
-                    pick(sums[i, rows, :], axis=1, keepdims=True), rows.start, lines[i]
-                )
-            own = turned[rows, :]
-            columns = [
-                jnp.broadcast_to(own[:, field : field + 1], (ROWS, size)) for field in OWN_FIELDS
-            ]
-            for i, column in enumerate(columns):
-                cols[i, rows, :] = column
-            for i, total in enumerate(summed(columns, sources, None)):
-                sums[i, rows, :] = total
+                for i, part in enumerate(parts):
+                    cols[i, rows, :] = part
+                columns.append(parts)
+            for rows, totals in zip(group, summed(columns, chosen, None)):
+                for i, total in enumerate(totals):
+                    sums[i, rows, :] = total
         lines = [jnp.sum(line, axis=0, keepdims=True) for line in lines]
         for i in range(3):
             accel_ref[i, pl.ds(prior, 1), :] = FORCE_NORM * lines[i]
@@ -215,12 +236,12 @@
         least_ref[...] = jnp.minimum(least_ref[...], step)
 
     def more_pass(chosen):
-        sources = read(chosen)
-        for rows in chunks:
-            columns = [cols[i, rows, :] for i in range(len(OWN_FIELDS))]
-            totals = [sums[i, rows, :] for i in range(5)]
-            for i, total in enumerate(summed(columns, sources, totals)):
-                sums[i, rows, :] = total
+        for group in grouped(size, 2):
+            columns = [[cols[i, rows, :] for i in range(len(OWN_FIELDS))] for rows in group]
+            totals = [[sums[i, rows, :] for i in range(5)] for rows in group]
+            for rows, total in zip(group, summed(columns, chosen, totals)):
+                for i in range(5):
+                    sums[i, rows, :] = total[i]
 
     sums[...] = jnp.zeros_like(sums)
     sweep(width, nbr_ref, count_ref, live_ref, prepare, first_pass, more_pass)
@@ -324,6 +345,7 @@
         in_specs=[smem, smem, smem, vmem],
         out_specs=vmem,
         scratch_shapes=[
+            pltpu.VMEM((slots, 4, ROWS, size), jnp.float32),
             pltpu.VMEM((size, table.shape[1]), jnp.float32),
             pltpu.VMEM((5, size, size), jnp.float32),
             pltpu.VMEM((size, size), jnp.float32),
@@ -343,6 +365,7 @@
         out_specs=[vmem, vmem, vmem],
         scratch_shapes=[
             pltpu.VMEM((slots, 16, size), jnp.float32),
+            pltpu.VMEM((slots, len(OWN_FIELDS) + 1, ROWS, size), jnp.float32),
             pltpu.VMEM((size, 16), jnp.float32),
             pltpu.VMEM((len(OWN_FIELDS), size, size), jnp.float32),
             pltpu.VMEM((5, size, size), jnp.float32),

time: 267 us -> 270 us (1.011); the launches traced: 266 us -> 272 us
  starting transfers between devices: 20.2 us -> 24.4 us
    ppermute x2, starting transfers between devices: 10.9 us -> 14.5 us  [spread(): before = lax.ppermute(blocks[send_list[0, peer_count + 1]], 'gx', up)]
where the time goes in v3:
time: 270 us; the launch traced here: 272 us
  Pallas kernels  218 us (81%)
  starting transfers between devices  24.4 us (9%)
  local copies, waits for them, and re-layouts  15.2 us (6%)
  waiting for transfers between devices  9.02 us (3%)
  other arithmetic  3.65 us (1%)
    pallas_call x1, Pallas kernels, shards(): pl.pallas_call(functools.partial(force_kernel, width), out_shape=[jax.Sha...  138 us
    pallas_call x1, Pallas kernels, shards(): pl.pallas_call(functools.partial(density_kernel, width), out_shape=square...  52.7 us
    pallas_call x1, Pallas kernels, least_of_all(): pl.pallas_call(functools.partial(least_kernel, axes), out_shape=jax.Shape...  27.9 us
    ppermute x2, starting transfers between devices, spread(): before = lax.ppermute(blocks[send_list[0, peer_count + 1]], 'gx', up)  14.5 us
    all_to_all x2, starting transfers between devices, spread(): lax.all_to_all(outgoing, 'gy', split_axis=0, concat_axis=0, tiled=True)  7.36 us
  transfers between devices with their start and end apart: 6, of which 3 were waited for; matrix products, arithmetic and copies ran while one was open for 2% of the time, Pallas kernels for 0%

profile of v3, /device:TPU:0, one launch (start us, length us, event | category | flops | bytes accessed | tf_op | source)
XLA Modules:
  0.0 271.9 jit_solution(16118179788950451015)
XLA Ops:
  0.6 0.0 copy-start.3
  0.6 0.7 fusion.1
  1.4 1.8 slice_bitcast_fusion
  3.2 2.4 stack.3
  5.6 0.0 copy-start.2
  5.6 0.6 gather_fusion.1
  6.2 4.9 %collective-permute-start = (f32[12,9,128]{2,1,0:T(8,128)S(1)}, f32[12,9,128]{2,1,0:T(8,128)S(1)}, u32[]{:S(2)}, u32[]{:S(2)}) collective-permute-start(f32[12,9,128]{2,1,0:T(8,128)S(1)} %gather_fusion.1), channel_id=1, source_target_pairs={{0,4},{4,8},{8,12},{12,16},{16,20},{20,24},{24,28},{1,5},{5,9},{9,... | collective-permute-start | bytes 165896 | tf_op jit(solution)/shard_map/ppermute | solution.py:314
  11.1 0.0 copy-done.3
  11.1 0.1 reshape_squeeze.4
  11.2 0.6 gather_fusion
  11.8 0.8 copy.14
  12.6 3.5 %all-to-all-start = ((f32[4,12,9,128]{3,1,2,0:T(8,128)}), f32[4,12,9,128]{3,1,2,0:T(8,128)S(1)}, u32[]{:S(2)}, u32[]{:S(2)}) async-start(f32[4,12,9,128]{3,1,2,0:T(8,128)} %copy.14), calls=%async_computation | async-start | bytes 589824 | tf_op jit(solution)/shard_map/all_to_all | solution.py:313
  16.1 0.6 gather_fusion.2
  16.7 1.3 collective-permute-start.1
  18.0 0.0 copy-done.2
  18.0 0.1 copy.13
  18.1 0.1 reshape.114.nbr_ref
  18.8 3.6 %all-to-all-done = f32[4,12,9,128]{3,1,2,0:T(8,128)S(1)} async-done(((f32[4,12,9,128]{3,1,2,0:T(8,128)}), f32[4,12,9,128]{3,1,2,0:T(8,128)S(1)}, u32[]{:S(2)}, u32[]{:S(2)}) %all-to-all-start) | async-done | bytes 221216 | tf_op jit(solution)/shard_map/all_to_all | solution.py:313
  22.4 0.1 copy.15
  22.5 0.0 collective-permute-done
  22.5 1.2 collective-permute-done.1
  23.7 0.0 copy-start.1
  23.7 0.1 pad_maximum_fusion.table_ref
  23.8 0.5 copy-done.1
  24.4 52.7 %density.1 = f32[128,128]{1,0:T(8,128)} custom-call(s32[1024]{0:T(1024)S(1)} %reshape.114.nbr_ref, s32[128]{0:T(128)S(1)} %copy-done.1, s32[1]{0:T(128)S(6)} %copy.19.live_ref, f32[200,9,128]{2,1,0:T(8,128)S(1)} %pad_maximum_fusion.table_ref), custom_call_target="tpu_custom_call" | custom-call | tf_op jit(solution)/shard_map/density/pallas_call | solution.py:342
  77.0 1.4 gather_fusion.3
  78.5 0.6 reshape.118
  79.1 3.9 %all-to-all-start.1 = ((f32[4,12,128]{2,1,0:T(8,128)}), f32[4,12,128]{2,1,0:T(8,128)S(1)}, u32[]{:S(2)}, u32[]{:S(2)}) async-start(f32[4,12,128]{2,1,0:T(8,128)} %reshape.118), calls=%async_computation.1 | async-start | bytes 65536 | tf_op jit(solution)/shard_map/all_to_all | solution.py:313
  83.0 1.4 gather_fusion.4
  84.4 1.4 gather_fusion.5
  85.8 9.6 %collective-permute-start.2 = (f32[12,128]{1,0:T(8,128)S(1)}, f32[12,128]{1,0:T(8,128)S(1)}, u32[]{:S(2)}, u32[]{:S(2)}) collective-permute-start(f32[12,128]{1,0:T(8,128)S(1)} %gather_fusion.4), channel_id=1, source_target_pairs={{0,4},{4,8},{8,12},{12,16},{16,20},{20,24},{24,28},{1,5},{5,9},{9,... | collective-permute-start | bytes 18440 | tf_op jit(solution)/shard_map/ppermute | solution.py:314
  95.4 1.3 collective-permute-start.3
  96.7 0.0 all-to-all-done.1
  96.8 0.0 collective-permute-done.2
  96.8 4.2 %collective-permute-done.3 = f32[12,128]{1,0:T(8,128)S(1)} collective-permute-done((f32[12,128]{1,0:T(8,128)S(1)}, f32[12,128]{1,0:T(8,128)S(1)}, u32[]{:S(2)}, u32[]{:S(2)}) %collective-permute-start.3) | collective-permute-done | bytes 6176 | tf_op jit(solution)/shard_map/ppermute | solution.py:315
  101.0 0.8 pad_maximum_fusion.1.rho_ref
  101.8 137.6 %force.1 = (f32[3,128,128]{2,1,0:T(8,128)S(1)}, f32[128,128]{1,0:T(8,128)S(1)}, f32[8,128]{1,0:T(8,128)S(1)}) custom-call(s32[1024]{0:T(1024)S(1)} %reshape.114.nbr_ref, s32[128]{0:T(128)S(1)} %copy-done.1, s32[1]{0:T(128)S(6)} %copy.19.live_ref, f32[200,9,128]{2,1,0:T(8,128)S(1)} %pad_maximum_fusion.table_ref, f32[200,128]{1,0:T(8,128)S(1)} %pad_maximum_fusion.1.rho_ref), custom_call_target="tpu_custom_call" | custom-call | tf_op jit(solution)/shard_map/force/pallas_call | solution.py:357
  239.4 0.0 copy-start
  239.4 0.6 copy-done
  240.0 27.9 %least_of_all.1 = f32[8,128]{1,0:T(8,128)} custom-call(f32[8,128]{1,0:T(8,128)} %copy-done), custom_call_target="tpu_custom_call" | custom-call | tf_op jit(solution)/shard_map/least_of_all/pallas_call | solution.py:296
  268.0 1.2 slice.42
  269.2 1.3 multiply_bitcast_fusion.1
  270.4 0.7 multiply_bitcast_fusion
  271.1 0.8 copy.18
  (6 shorter events, 0.1 us)
Async XLA Ops:
  0.6 10.5 %copy-start.3 = (s32[1,6,12]{2,0,1:T(1,128)S(1)}, s32[1,6,12]{2,0,1:T(1,128)}, u32[]{:S(2)}) copy-start(s32[1,6,12]{2,0,1:T(1,128)} %param.15) | copy-start | bytes 868
  5.6 12.3 %copy-start.2 = (s32[128,8]{0,1:T(8,128)S(1)}, s32[128,8]{0,1:T(8,128)}, u32[]{:S(2)}) copy-start(s32[128,8]{0,1:T(8,128)} %param.16) | copy-start | bytes 12292
  6.2 16.3 %collective-permute-start = (f32[12,9,128]{2,1,0:T(8,128)S(1)}, f32[12,9,128]{2,1,0:T(8,128)S(1)}, u32[]{:S(2)}, u32[]{:S(2)}) collective-permute-start(f32[12,9,128]{2,1,0:T(8,128)S(1)} %gather_fusion.1), channel_id=1, source_target_pairs={{0,4},{4,8},{8,12},{12,16},{16,20},{20,24},{24,28},{1,5},{5,9},{9,... | collective-permute-start | bytes 165896 | tf_op jit(solution)/shard_map/ppermute | solution.py:314
  12.6 9.8 %all-to-all-start = ((f32[4,12,9,128]{3,1,2,0:T(8,128)}), f32[4,12,9,128]{3,1,2,0:T(8,128)S(1)}, u32[]{:S(2)}, u32[]{:S(2)}) async-start(f32[4,12,9,128]{3,1,2,0:T(8,128)} %copy.14), calls=%async_computation | async-start | bytes 589824 | tf_op jit(solution)/shard_map/all_to_all | solution.py:313
  16.7 7.1 %collective-permute-start.1 = (f32[12,9,128]{2,1,0:T(8,128)S(1)}, f32[12,9,128]{2,1,0:T(8,128)S(1)}, u32[]{:S(2)}, u32[]{:S(2)}) collective-permute-start(f32[12,9,128]{2,1,0:T(8,128)S(1)} %gather_fusion.2), channel_id=1, source_target_pairs={{4,0},{8,4},{12,8},{16,12},{20,16},{24,20},{28,24},{5,1},{9,5},{13... | collective-permute-start | bytes 165896 | tf_op jit(solution)/shard_map/ppermute | solution.py:315
  23.7 0.7 copy-start.1
  79.1 17.6 %all-to-all-start.1 = ((f32[4,12,128]{2,1,0:T(8,128)}), f32[4,12,128]{2,1,0:T(8,128)S(1)}, u32[]{:S(2)}, u32[]{:S(2)}) async-start(f32[4,12,128]{2,1,0:T(8,128)} %reshape.118), calls=%async_computation.1 | async-start | bytes 65536 | tf_op jit(solution)/shard_map/all_to_all | solution.py:313
  85.8 11.0 %collective-permute-start.2 = (f32[12,128]{1,0:T(8,128)S(1)}, f32[12,128]{1,0:T(8,128)S(1)}, u32[]{:S(2)}, u32[]{:S(2)}) collective-permute-start(f32[12,128]{1,0:T(8,128)S(1)} %gather_fusion.4), channel_id=1, source_target_pairs={{0,4},{4,8},{8,12},{12,16},{16,20},{20,24},{24,28},{1,5},{5,9},{9,... | collective-permute-start | bytes 18440 | tf_op jit(solution)/shard_map/ppermute | solution.py:314
  95.4 5.5 %collective-permute-start.3 = (f32[12,128]{1,0:T(8,128)S(1)}, f32[12,128]{1,0:T(8,128)S(1)}, u32[]{:S(2)}, u32[]{:S(2)}) collective-permute-start(f32[12,128]{1,0:T(8,128)S(1)} %gather_fusion.5), channel_id=1, source_target_pairs={{4,0},{8,4},{12,8},{16,12},{20,16},{24,20},{28,24},{5,1},{9,5},{13... | collective-permute-start | bytes 18440 | tf_op jit(solution)/shard_map/ppermute | solution.py:315
  239.4 0.6 copy-start

commit v4 on v2

--- a/solution.py
+++ b/solution.py
@@ -37,39 +37,58 @@
     return row + jnp.where(lanes == sublanes + first, column, 0.0)
 
 
-def sweep(width, nbr_ref, count_ref, live_ref, prepare, first_pass, more_pass):
-    live = live_ref[0]
-    prepare(0)
+def sweep(width, wanted, nbr_ref, count_ref, live_ref, flag_ref, order, steps):
+    prepare, head, more_pass, least_done = steps
+
+    def fill(block, n):
+        order[n] = block
+        return n + jnp.where(flag_ref[block] == wanted, 1, 0)
+
+    chosen = lax.fori_loop(0, live_ref[0], fill, 0)
 
     def turn(i, carry):
-        block = jnp.minimum(i, live - 1)
-        after = jnp.minimum(i + 1, live - 1)
-        prior = jnp.maximum(i - 1, 0)
+        block = order[jnp.minimum(i, chosen - 1)]
+        after = order[jnp.minimum(i + 1, chosen - 1)]
+        prior = order[jnp.maximum(i - 1, 0)]
         base = block * width
-        count = count_ref[block]
-        odd = lax.rem(count - SURE, 2)
-        for extra in range(2):
-
-            @pl.when(odd == extra)
+        count = jnp.where(i < chosen, count_ref[block], 0)
+        odd = lax.rem(count, 2)
+        if least_done:
+            for extra in range(2):
+
+                @pl.when(odd == extra)
+                def _():
+                    head([nbr_ref[base + j] for j in range(least_done + extra)], prior)
+                    prepare(after)
+
+        else:
+            head([], prior)
+            prepare(after)
+
+            @pl.when(odd == 1)
             def _():
-                first_pass([nbr_ref[base + j] for j in range(SURE + extra)], prior)
-                prepare(after)
-
-        done = SURE + odd
+                more_pass([nbr_ref[base]])
+
+        done = least_done + odd
 
         def more(j, carry):
             at = base + done + 2 * j
             more_pass([nbr_ref[at], nbr_ref[at + 1]])
             return carry
 
-        return lax.fori_loop(0, (count - done) // 2, more, carry)
-
-    lax.fori_loop(0, live + 1, turn, 0)
-
-
-def density_kernel(width, nbr_ref, count_ref, live_ref, table_ref, rho_ref, turned, cols, sums):
+        return lax.fori_loop(0, lax.div(jnp.maximum(count - done, 0), 2), more, carry)
+
+    @pl.when(chosen > 0)
+    def _():
+        prepare(order[0])
+        lax.fori_loop(0, chosen + 1, turn, 0)
+
+
+def density_kernel(width, wanted, *refs):
+    *lists, table_ref = refs[:5]
+    rho_ref, order, turned, cols, sums = refs[-5:]
     size = table_ref.shape[2]
-    rho_ref[...] = jnp.zeros_like(rho_ref)
+    rho_ref[...] = refs[5][...] if wanted else jnp.zeros_like(rho_ref)
     chunks = [pl.ds(first, ROWS) for first in range(0, size, ROWS)]
 
     def prepare(block):
@@ -116,29 +135,21 @@
             columns = [cols[i, rows, :] for i in range(5)]
             sums[rows, :] = summed(columns, sources, sums[rows, :])
 
-    sweep(width, nbr_ref, count_ref, live_ref, prepare, first_pass, more_pass)
-
-
-def force_kernel(
-    width,
-    nbr_ref,
-    count_ref,
-    live_ref,
-    table_ref,
-    rho_ref,
-    accel_ref,
-    rate_ref,
-    least_ref,
-    full,
-    turned,
-    cols,
-    sums,
-):
+    sweep(width, wanted, *lists, order, (prepare, first_pass, more_pass, SURE))
+
+
+def force_kernel(width, wanted, *refs):
+    *lists, table_ref, rho_ref = refs[:6]
+    accel_ref, rate_ref, least_ref, order, full, turned, cols, sums = refs[-8:]
     size = table_ref.shape[2]
     slots = table_ref.shape[0]
-    accel_ref[...] = jnp.zeros_like(accel_ref)
-    rate_ref[...] = jnp.zeros_like(rate_ref)
-    least_ref[...] = jnp.full(least_ref.shape, FAR_STEP, jnp.float32)
+    if wanted:
+        for ref, part in zip((accel_ref, rate_ref, least_ref), refs[6:9]):
+            ref[...] = part[...]
+    else:
+        accel_ref[...] = jnp.zeros_like(accel_ref)
+        rate_ref[...] = jnp.zeros_like(rate_ref)
+        least_ref[...] = jnp.full(least_ref.shape, FAR_STEP, jnp.float32)
     chunks = [pl.ds(first, ROWS) for first in range(0, size, ROWS)]
 
     def derive(turn, carry):
@@ -188,7 +199,6 @@
         return totals
 
     def first_pass(chosen, prior):
-        sources = read(chosen)
         lines = [jnp.zeros((ROWS, size), jnp.float32) for _ in range(5)]
         for rows in chunks:
             for i in range(5):
@@ -202,8 +212,8 @@
             ]
             for i, column in enumerate(columns):
                 cols[i, rows, :] = column
-            for i, total in enumerate(summed(columns, sources, None)):
-                sums[i, rows, :] = total
+            for i in range(5):
+                sums[i, rows, :] = jnp.zeros((ROWS, size), jnp.float32)
         lines = [jnp.sum(line, axis=0, keepdims=True) for line in lines]
         for i in range(3):
             accel_ref[i, pl.ds(prior, 1), :] = FORCE_NORM * lines[i]
@@ -223,7 +233,7 @@
                 sums[i, rows, :] = total
 
     sums[...] = jnp.zeros_like(sums)
-    sweep(width, nbr_ref, count_ref, live_ref, prepare, first_pass, more_pass)
+    sweep(width, wanted, *lists, order, (prepare, first_pass, more_pass, 0))
     least = jnp.min(least_ref[...], axis=1, keepdims=True)
     least_ref[...] = jnp.broadcast_to(least, least_ref.shape)
 
@@ -311,45 +321,58 @@
         + [cut(energy)],
         axis=1,
     )
-    table = jnp.concatenate([own] + spread(own, send_list, ny, slot_count), axis=0)
-    slots = table.shape[0]
-    lists = nbr_list.reshape(-1)
+    ghosts = spread(own, send_list, ny, slot_count)
+    used = jnp.arange(width, dtype=jnp.int32)[None, :] < nbr_count[:, None]
+    flags = jnp.any(used & (nbr_list >= block_count), axis=1).astype(jnp.int32)
+    lists = (nbr_list.reshape(-1), nbr_count, live_blocks, flags)
     smem = pl.BlockSpec(memory_space=pltpu.SMEM)
     vmem = pl.BlockSpec(memory_space=pltpu.VMEM)
-    params = pltpu.CompilerParams(vmem_limit_bytes=VMEM_BYTES)
     square = jax.ShapeDtypeStruct((block_count, size), jnp.float32)
-    rho = pl.pallas_call(
-        functools.partial(density_kernel, width),
-        out_shape=square,
-        in_specs=[smem, smem, smem, vmem],
-        out_specs=vmem,
-        scratch_shapes=[
-            pltpu.VMEM((size, table.shape[1]), jnp.float32),
-            pltpu.VMEM((5, size, size), jnp.float32),
-            pltpu.VMEM((size, size), jnp.float32),
-        ],
-        compiler_params=params,
-        name="density",
-    )(lists, nbr_count, live_blocks, table)
-    wide_rho = jnp.concatenate([rho] + spread(rho, send_list, ny, slot_count), axis=0)
-    accel, rate, least = pl.pallas_call(
-        functools.partial(force_kernel, width),
-        out_shape=[
-            jax.ShapeDtypeStruct((3, block_count, size), jnp.float32),
-            square,
-            jax.ShapeDtypeStruct((8, 128), jnp.float32),
-        ],
-        in_specs=[smem, smem, smem, vmem, vmem],
-        out_specs=[vmem, vmem, vmem],
-        scratch_shapes=[
+    pairs = block_count * width * size * size
+
+    def call(kernel, wanted, name, out, scratch, flops, *operands):
+        return pl.pallas_call(
+            functools.partial(kernel, width, wanted),
+            out_shape=out,
+            in_specs=[smem] * len(lists) + [vmem] * len(operands),
+            out_specs=jax.tree.map(lambda _: vmem, out),
+            scratch_shapes=[pltpu.SMEM((block_count,), jnp.int32)] + scratch,
+            compiler_params=pltpu.CompilerParams(vmem_limit_bytes=VMEM_BYTES),
+            cost_estimate=pl.CostEstimate(
+                flops=flops * pairs, bytes_accessed=4 * own.size, transcendentals=pairs
+            ),
+            name=name,
+        )(*lists, *operands)
+
+    scratch = [
+        pltpu.VMEM((size, own.shape[1]), jnp.float32),
+        pltpu.VMEM((5, size, size), jnp.float32),
+        pltpu.VMEM((size, size), jnp.float32),
+    ]
+    inner = call(density_kernel, 0, "density_inner", square, scratch, 18, own)
+    table = jnp.concatenate([own] + ghosts, axis=0)
+    rho = call(density_kernel, 1, "density_edge", square, scratch, 18, table, inner)
+    ghosts = spread(rho, send_list, ny, slot_count)
+    out = [
+        jax.ShapeDtypeStruct((3, block_count, size), jnp.float32),
+        square,
+        jax.ShapeDtypeStruct((8, 128), jnp.float32),
+    ]
+
+    def room(slots):
+        return [
             pltpu.VMEM((slots, 16, size), jnp.float32),
             pltpu.VMEM((size, 16), jnp.float32),
             pltpu.VMEM((len(OWN_FIELDS), size, size), jnp.float32),
             pltpu.VMEM((5, size, size), jnp.float32),
-        ],
-        compiler_params=params,
-        name="force",
-    )(lists, nbr_count, live_blocks, table, wide_rho)
+        ]
+
+    inner = call(force_kernel, 0, "force_inner", out, room(block_count), 50, own, rho)
+    wide_rho = jnp.concatenate([rho] + ghosts, axis=0)
+    slots = table.shape[0]
+    accel, rate, least = call(
+        force_kernel, 1, "force_edge", out, room(slots), 50, table, wide_rho, *inner
+    )
     timestep = least_of_all(least, (("gy", ny), ("gx", nx)))[0, 0]
     return (rho.reshape(-1), (timestep * accel).reshape(3, -1), (timestep * rate).reshape(-1))
 

time: 267 us -> 312 us (1.17)
  Pallas kernels: 216 us -> 247 us
  starting transfers between devices: 20.2 us -> 44.5 us
  waiting for transfers between devices: 9.02 us -> 0.02 us
    pallas_call x1, Pallas kernels: 29.3 us -> 102 us  [least_of_all(): pl.pallas_call(functools.partial(least_kernel, axes), out_shape=jax.Shape...]
    pallas_call x2 -> x4, Pallas kernels: 187 us -> 145 us  [call(): pl.pallas_call(functools.partial(kernel, width, wanted), out_shape=out, i...]
    all_to_all x2, starting transfers between devices: 6.71 us -> 31 us  [spread(): lax.all_to_all(outgoing, 'gy', split_axis=0, concat_axis=0, tiled=True)]
    ppermute x2, waiting for transfers between devices: 5.38 us -> 0.01 us  [spread(): after = lax.ppermute(blocks[send_list[0, peer_count]], 'gx', down)]
    all_to_all x2, waiting for transfers between devices: 3.62 us -> 0.01 us  [spread(): lax.all_to_all(outgoing, 'gy', split_axis=0, concat_axis=0, tiled=True)]
  transfers between devices with their start and end apart: 6 -> 6, of which waited for: 3 -> 0; matrix products, arithmetic and copies ran while one was open for 2% -> 1% of each run, Pallas kernels for 0% -> 29%
where the time goes in v4:
time: 312 us; the launch traced here: 311 us
  Pallas kernels  247 us (79%)
  starting transfers between devices  44.5 us (14%)
  local copies, waits for them, and re-layouts  15.5 us (5%)
    pallas_call x4, Pallas kernels, call(): pl.pallas_call(functools.partial(kernel, width, wanted), out_shape=out, i...  145 us
    pallas_call x1, Pallas kernels, least_of_all(): pl.pallas_call(functools.partial(least_kernel, axes), out_shape=jax.Shape...  102 us
    all_to_all x2, starting transfers between devices, spread(): lax.all_to_all(outgoing, 'gy', split_axis=0, concat_axis=0, tiled=True)  31 us
    ppermute x2, starting transfers between devices, spread(): before = lax.ppermute(blocks[send_list[0, peer_count + 1]], 'gx', up)  10.9 us
  transfers between devices with their start and end apart: 6, of which 0 were waited for; matrix products, arithmetic and copies ran while one was open for 1% of the time, Pallas kernels for 29%

profile of v4, /device:TPU:0, one launch (start us, length us, event | category | flops | bytes accessed | tf_op | source)
XLA Modules:
  0.0 311.2 jit_solution(17748939860477130436)
XLA Ops:
  0.6 0.0 copy-start.5
  0.6 0.7 fusion.3
  1.4 1.8 slice_bitcast_fusion
  3.2 2.4 stack.3.refs_4_
  5.6 0.0 copy-start.3
  5.6 0.0 copy-start.4
  5.7 0.6 gather_fusion.1
  6.2 4.9 %collective-permute-start = (f32[12,9,128]{2,1,0:T(8,128)S(1)}, f32[12,9,128]{2,1,0:T(8,128)S(1)}, u32[]{:S(2)}, u32[]{:S(2)}) collective-permute-start(f32[12,9,128]{2,1,0:T(8,128)S(1)} %gather_fusion.1), channel_id=1, source_target_pairs={{0,4},{4,8},{8,12},{12,16},{16,20},{20,24},{24,28},{1,5},{5,9},{9,... | collective-permute-start | bytes 165896 | tf_op jit(solution)/shard_map/ppermute | solution.py:303
  11.1 0.0 copy-done.5
  11.1 0.1 reshape_squeeze.4
  11.2 0.6 gather_fusion
  11.9 0.8 copy.14
  12.7 3.5 %all-to-all-start = ((f32[4,12,9,128]{3,1,2,0:T(8,128)}), f32[4,12,9,128]{3,1,2,0:T(8,128)S(1)}, u32[]{:S(2)}, u32[]{:S(2)}) async-start(f32[4,12,9,128]{3,1,2,0:T(8,128)} %copy.14), calls=%async_computation | async-start | bytes 589824 | tf_op jit(solution)/shard_map/all_to_all | solution.py:302
  16.1 0.6 gather_fusion.2
  16.7 1.3 collective-permute-start.1
  18.0 0.0 copy-done.3
  18.0 0.0 copy-done.4
  18.0 0.1 copy.13
  18.1 0.1 reshape.115.refs_0_
  18.9 20.2 %density_inner.1.refs_5_ = f32[128,128]{1,0:T(8,128)S(1)} custom-call(s32[1024]{0:T(1024)S(1)} %reshape.115.refs_0_, s32[128]{0:T(128)S(1)} %copy-done.3, s32[1]{0:T(128)S(6)} %copy.19.refs_2_, s32[128]{0:T(128)S(1)} %convert_element_type.3.refs_3_, f32[128,9,128]{2,1,0:T(8,128)S(1)} %stack.3.refs_4_), custom_call_target="tpu_custom_call" | custom-call | flops 301989888 | bytes 589824 | tf_op jit(solution)/shard_map/density_inner/pallas_call | solution.py:334
  39.1 0.0 all-to-all-done
  39.1 0.1 copy.15
  39.2 0.0 collective-permute-done
  39.2 0.0 collective-permute-done.1
  39.2 0.1 pad_maximum_fusion.refs_4_
  39.3 13.4 %density_edge.1.refs_5_ = f32[128,128]{1,0:T(8,128)} custom-call(s32[1024]{0:T(1024)S(1)} %reshape.115.refs_0_, s32[128]{0:T(128)S(1)} %copy-done.3, s32[1]{0:T(128)S(6)} %copy.19.refs_2_, s32[128]{0:T(128)S(1)} %convert_element_type.3.refs_3_, f32[200,9,128]{2,1,0:T(8,128)S(1)} %pad_maximum_fusion.refs_4_, f32[128,128]{1,0:T(8,128)S(1)} %density_inner.1.refs_5_), custom_call_target="tpu_custom_call" | custom-call | flops 301989888 | bytes 589824 | tf_op jit(solution)/shard_map/density_edge/pallas_call | solution.py:334
  52.7 1.4 gather_fusion.3
  54.1 1.4 gather_fusion.4
  55.5 1.4 gather_fusion.5
  56.9 0.6 reshape.119
  57.5 0.0 copy-start.1
  57.5 27.5 %all-to-all-start.1 = ((f32[4,12,128]{2,1,0:T(8,128)}), f32[4,12,128]{2,1,0:T(8,128)S(1)}, u32[]{:S(2)}, u32[]{:S(2)}) async-start(f32[4,12,128]{2,1,0:T(8,128)} %reshape.119), calls=%async_computation.1 | async-start | bytes 65536 | tf_op jit(solution)/shard_map/all_to_all | solution.py:302
  85.0 6.0 %collective-permute-start.2 = (f32[12,128]{1,0:T(8,128)S(1)}, f32[12,128]{1,0:T(8,128)S(1)}, u32[]{:S(2)}, u32[]{:S(2)}) collective-permute-start(f32[12,128]{1,0:T(8,128)S(1)} %gather_fusion.4), channel_id=1, source_target_pairs={{0,4},{4,8},{8,12},{12,16},{16,20},{20,24},{24,28},{1,5},{5,9},{9,... | collective-permute-start | bytes 18440 | tf_op jit(solution)/shard_map/ppermute | solution.py:303
  91.1 1.3 collective-permute-start.3
  92.4 0.0 copy-start
  92.4 0.8 copy-done
  93.2 69.2 %force_inner.1 = (f32[3,128,128]{2,1,0:T(8,128)S(1)}, f32[128,128]{1,0:T(8,128)S(1)}, f32[8,128]{1,0:T(8,128)S(1)}) custom-call(s32[1024]{0:T(1024)S(1)} %reshape.115.refs_0_, s32[128]{0:T(128)S(1)} %copy-done.3, s32[1]{0:T(128)S(6)} %copy.19.refs_2_, s32[128]{0:T(128)S(1)} %convert_element_type.3.refs_3_, f32[128,9,128]{2,1,0:T(8,128)S(1)} %stack.3.refs_4_, ...), custom_call_target="tpu_custom_call" | custom-call | flops 838860800 | bytes 589824 | tf_op jit(solution)/shard_map/force_inner/pallas_call | solution.py:334
  162.4 0.0 all-to-all-done.1
  162.4 0.0 collective-permute-done.2
  162.4 0.0 collective-permute-done.3
  162.4 0.0 copy-done.1
  162.5 42.4 %force_edge.1 = (f32[3,128,128]{2,1,0:T(8,128)S(1)}, f32[128,128]{1,0:T(8,128)S(1)}, f32[8,128]{1,0:T(8,128)S(1)}) custom-call(s32[1024]{0:T(1024)S(1)} %reshape.115.refs_0_, s32[128]{0:T(128)S(1)} %copy-done.3, s32[1]{0:T(128)S(6)} %copy.19.refs_2_, s32[128]{0:T(128)S(1)} %convert_element_type.3.refs_3_, f32[200,9,128]{2,1,0:T(8,128)S(1)} %pad_maximum_fusion.refs_4_, ...), custom_call_target="tpu_custom_call" | custom-call | flops 838860800 | bytes 589824 | tf_op jit(solution)/shard_map/force_edge/pallas_call | solution.py:334
  204.9 0.0 copy-start.2
  204.9 0.6 copy-done.2
  205.5 101.8 %least_of_all.1 = f32[8,128]{1,0:T(8,128)} custom-call(f32[8,128]{1,0:T(8,128)} %copy-done.2), custom_call_target="tpu_custom_call" | custom-call | tf_op jit(solution)/shard_map/least_of_all/pallas_call | solution.py:285
  307.2 1.2 slice.42
  308.4 1.3 multiply_bitcast_fusion.1
  309.7 0.7 multiply_bitcast_fusion
  310.4 0.8 copy.18
  (9 shorter events, 0.1 us)
Async XLA Ops:
  0.6 10.5 %copy-start.5 = (s32[1,6,12]{2,0,1:T(1,128)S(1)}, s32[1,6,12]{2,0,1:T(1,128)}, u32[]{:S(2)}) copy-start(s32[1,6,12]{2,0,1:T(1,128)} %param.15) | copy-start | bytes 868
  5.6 12.4 %copy-start.3 = (s32[128]{0:T(128)S(1)}, s32[128]{0:T(128)}, u32[]{:S(2)}) copy-start(s32[128]{0:T(128)} %refs_1_.7) | copy-start | bytes 1540
  5.6 12.4 %copy-start.4 = (s32[128,8]{0,1:T(8,128)S(1)}, s32[128,8]{0,1:T(8,128)}, u32[]{:S(2)}) copy-start(s32[128,8]{0,1:T(8,128)} %param.16) | copy-start | bytes 12292
  6.2 32.9 %collective-permute-start = (f32[12,9,128]{2,1,0:T(8,128)S(1)}, f32[12,9,128]{2,1,0:T(8,128)S(1)}, u32[]{:S(2)}, u32[]{:S(2)}) collective-permute-start(f32[12,9,128]{2,1,0:T(8,128)S(1)} %gather_fusion.1), channel_id=1, source_target_pairs={{0,4},{4,8},{8,12},{12,16},{16,20},{20,24},{24,28},{1,5},{5,9},{9,... | collective-permute-start | bytes 165896 | tf_op jit(solution)/shard_map/ppermute | solution.py:303
  12.7 26.4 %all-to-all-start = ((f32[4,12,9,128]{3,1,2,0:T(8,128)}), f32[4,12,9,128]{3,1,2,0:T(8,128)S(1)}, u32[]{:S(2)}, u32[]{:S(2)}) async-start(f32[4,12,9,128]{3,1,2,0:T(8,128)} %copy.14), calls=%async_computation | async-start | bytes 589824 | tf_op jit(solution)/shard_map/all_to_all | solution.py:302
  16.7 22.5 %collective-permute-start.1 = (f32[12,9,128]{2,1,0:T(8,128)S(1)}, f32[12,9,128]{2,1,0:T(8,128)S(1)}, u32[]{:S(2)}, u32[]{:S(2)}) collective-permute-start(f32[12,9,128]{2,1,0:T(8,128)S(1)} %gather_fusion.2), channel_id=1, source_target_pairs={{4,0},{8,4},{12,8},{16,12},{20,16},{24,20},{28,24},{5,1},{9,5},{13... | collective-permute-start | bytes 165896 | tf_op jit(solution)/shard_map/ppermute | solution.py:304
  57.5 104.9 %copy-start.1 = (f32[128,128]{1,0:T(8,128)S(1)}, f32[128,128]{1,0:T(8,128)}, u32[]{:S(2)}) copy-start(f32[128,128]{1,0:T(8,128)} %density_edge.1.refs_5_) | copy-start | bytes 196612
  57.5 104.9 %all-to-all-start.1 = ((f32[4,12,128]{2,1,0:T(8,128)}), f32[4,12,128]{2,1,0:T(8,128)S(1)}, u32[]{:S(2)}, u32[]{:S(2)}) async-start(f32[4,12,128]{2,1,0:T(8,128)} %reshape.119), calls=%async_computation.1 | async-start | bytes 65536 | tf_op jit(solution)/shard_map/all_to_all | solution.py:302
  85.0 77.4 %collective-permute-start.2 = (f32[12,128]{1,0:T(8,128)S(1)}, f32[12,128]{1,0:T(8,128)S(1)}, u32[]{:S(2)}, u32[]{:S(2)}) collective-permute-start(f32[12,128]{1,0:T(8,128)S(1)} %gather_fusion.4), channel_id=1, source_target_pairs={{0,4},{4,8},{8,12},{12,16},{16,20},{20,24},{24,28},{1,5},{5,9},{9,... | collective-permute-start | bytes 18440 | tf_op jit(solution)/shard_map/ppermute | solution.py:303
  91.1 71.4 %collective-permute-start.3 = (f32[12,128]{1,0:T(8,128)S(1)}, f32[12,128]{1,0:T(8,128)S(1)}, u32[]{:S(2)}, u32[]{:S(2)}) collective-permute-start(f32[12,128]{1,0:T(8,128)S(1)} %gather_fusion.5), channel_id=1, source_target_pairs={{4,0},{8,4},{12,8},{16,12},{20,16},{24,20},{28,24},{5,1},{9,5},{13... | collective-permute-start | bytes 18440 | tf_op jit(solution)/shard_map/ppermute | solution.py:304
  92.4 0.8 copy-start
  204.9 0.6 copy-start.2
